TPU v7x, 128 devices: a whole 4x4x4 slice. The times are simulated.
128 devices in a mesh: gx: 16 (over x, y), gy: 8 (over z, core).
Axes of the slice: x: 4, y: 4, z: 4, core: 2. Of those that a mesh axis runs over, the one named last changes fastest.
Arguments:
- adj_head: float32 [256, 256, 256], P('gx', 'gy'), may hold values from -6 to 6
- adj_species: float32 [6, 256, 256, 256], P(None, 'gx', 'gy'), may hold values from -6 to 6
- cond: float32 [256, 256, 256], P('gx', 'gy'), may hold values from 0.1 to 1
- capacity: float32 [256, 256, 256], P('gx', 'gy'), may hold values from 0.5 to 2
- rate: float32 [256, 256, 256], P('gx', 'gy'), may hold values from 0.1 to 1
- diffusion: float32 [6], replicated, may hold values from 0.05 to 0.3
- coupling: float32 [6], replicated, may hold values from -3 to 3
- react: float32 [4, 6, 6], replicated, may hold values from -6 to 6
- material: int32 [256, 256, 256], P('gx', 'gy'), may hold values from 0 to 3
- drain_mask: int32 [256, 256, 256], P('gx', 'gy'), may hold values 0 or 1
- block_pipe: int32 [256, 256, 2], P('gx', 'gy'), may hold values from 0 to 255
- pipe_obs: float32 [7, 16, 256], P(None, 'gx', 'gy'), may hold values from -6 to 6
Outputs:
- head_out: float32 [256, 256, 256], P('gx', 'gy')
- species_out: float32 [6, 256, 256, 256], P(None, 'gx', 'gy')
All inputs are finite; a program needn't handle non-finite values. No bound on the sum of `drain_mask` on one device may be relied on, other than what follows from the above.
Results may differ from a plain program's by a relative error of at most 0.0003.
Values sent between devices are 32-bit elements; how exact they have to be, the bound alone decides.
No kernel may reach another device: no remote copies, remote signals or barrier semaphores. Data moves between devices by JAX's collectives and lax.ppermute only.
A program may use at most 128 MiB of HBM per device.

v0:
```python
import functools

import jax
import jax.numpy as jnp
from jax import lax
from jax.experimental import pallas as pl
from jax.experimental.pallas import tpu as pltpu
from jax.sharding import PartitionSpec as P

ITERS = 3
time_step = 0.08
drain_gain = 0.5

F32 = jnp.float32
BF16 = jnp.bfloat16
HB = pl.BlockSpec(memory_space=pltpu.HBM)
ANY = pl.BlockSpec(memory_space=pl.ANY)
VM = pl.BlockSpec(memory_space=pltpu.VMEM)
SM = pl.BlockSpec(memory_space=pltpu.SMEM)
TOP = 8
STEP = 4
RB = 16


VLIM = 18 * 2**20
LANES = (slice(0, 128), slice(128, 256))


def split(x, pieces):
    out = []
    for _ in range(pieces):
        piece = x.astype(BF16)
        out.append(piece)
        x = x - piece.astype(F32)
    return out


def block_onehot(bp, block, n_pipes):
    col = bp[:, :, block : block + 1]
    col = col.reshape(col.shape[0] * col.shape[1], 1)
    return (col == lax.broadcasted_iota(jnp.int32, (col.shape[0], n_pipes), 1)).astype(BF16)


def turn(x, by):
    return pltpu.roll(x, (-by) % 128, 1)


def halve(values):
    low = lax.broadcasted_iota(jnp.int32, values[0].shape, 1) < 64
    return [
        jnp.where(low, a, b) + turn(jnp.where(low, b, a), 64)
        for a, b in zip(values[::2], values[1::2])
    ]


def merge(level):
    lane = lax.broadcasted_iota(jnp.int32, level[0].shape, 1)
    for width in (32, 16):
        low = lane & width == 0
        level = [
            jnp.where(low, a, b) + jnp.where(low, turn(a, width), turn(b, -width))
            for a, b in zip(level[::2], level[1::2])
        ]
    return level[0]


SUM_LANE = [64 * (c & 1) + 32 * (c >> 1 & 1) + 16 * (c >> 2 & 1) for c in range(8)]
CHUNK = 128


def block_sums(half, j):
    lane = lax.broadcasted_iota(jnp.int32, (16, 128), 1) // 16
    chan = lax.broadcasted_iota(jnp.int32, (16, 128), 0)
    group = 4 * (chan & 1) + 2 * (chan >> 1 & 1) + (chan >> 2 & 1)
    pick = ((lane == group) & (chan < 8)).astype(BF16)
    out = []
    for r in range(0, half.shape[2], CHUNK):
        merged = merge([half[j, c, r : r + CHUNK, :] for c in range(4)])
        total = None
        for piece in split(merged, 3)[::-1]:
            part = lax.dot_general(
                pick, piece, (((1,), (1,)), ((), ())), preferred_element_type=F32
            )
            total = part if total is None else total + part
        out.append(total)
    return jnp.concatenate(out, axis=1)[:8]


def pipe_sums(half, hot):
    total = None
    for j in range(2):
        rows = block_sums(half, j)
        stack = jnp.concatenate(split(rows, 3) + [jnp.zeros(rows.shape, BF16)], axis=0)
        part = jnp.dot(stack, hot[j], preferred_element_type=F32)
        total = part if total is None else total + part
    return (total[16:24] + total[8:16]) + total[:8]


def edge_flags():
    gx, gy = lax.axis_index("gx"), lax.axis_index("gy")
    return gx % 2 == 0, gy % 2 == 0, gy


def edges(h, sp, cond, cap):
    nx = h.shape[0]
    even = lax.axis_index("gx") % 2 == 0

    def pack(x):
        plane = lambda a, dim: lax.dynamic_slice_in_dim(a, x, 1, axis=dim)
        scaled = time_step * plane(h, 0) / plane(cap, 0)
        return jnp.concatenate([scaled, plane(sp, 1)[:, 0], plane(cond, 0)], axis=0)

    return pack(jnp.where(even, nx - 1, 0)), pack(jnp.where(even, 0, nx - 1))


def clear_rim(ref, nx, rows, *lead):
    tile = jnp.zeros((TOP, 128), F32)
    for j in range(2):
        for x in (0, nx + 1):
            for r in range(0, rows + 2 * TOP, TOP):
                ref[(j, *lead, x, slice(r, r + TOP))] = tile


def first_kernel(
    nx, rows, chans, h, sp, cond, cap, mask, bp, obs, st, kc, pa, pb, hot, half, whalf, vh, vcap, vmask, sem
):
    _, even_y, gy = edge_flags()
    nsp = chans - 1
    n_pipes = pa.shape[2]
    inside = pl.ds(TOP, rows)

    def chunk(g):
        at, into = pl.ds(g * STEP, STEP), pl.ds(g * STEP + 1, STEP)
        pairs = []
        for j in range(2):
            part = pl.ds(128 * j, 128)
            pairs.append((sp.at[:, at, :, part], st.at[j, pl.ds(1, nsp), into, inside, :]))
            pairs.append((cond.at[at, :, part], kc.at[j, into, inside, :]))
        for src, dst in ((h, vh), (cap, vcap), (mask, vmask)):
            pairs.append((src.at[at], dst.at[at]))
        return [pltpu.make_async_copy(a, b, sem.at[g, n]) for n, (a, b) in enumerate(pairs)]

    for g in range(nx // STEP):
        for copy in chunk(g):
            copy.start()
    for j in range(2):
        hot[j] = block_onehot(bp[...], j, n_pipes)
    for c in range(chans):
        clear_rim(st, nx, rows, c)
    clear_rim(kc, nx, rows)
    rim = jnp.zeros((TOP, 128), F32)
    low = lax.broadcasted_iota(jnp.int32, (rows, 128), 1) < 64

    def plane(x, carry):
        @pl.when(x % STEP == 0)
        def _():
            for copy in chunk(x // STEP):
                copy.wait()

        for j, part in enumerate(LANES):
            cd = kc[j, x + 1, TOP : TOP + rows, :]
            head = vh[x, :, part]
            m = vmask[x, :, part].astype(F32)
            scaled = time_step * head / vcap[x, :, part]
            st[j, 0, x + 1, TOP : TOP + rows, :] = scaled
            species = [st[j, c, x + 1, TOP : TOP + rows, :] for c in range(1, chans)]
            for c in range(chans):
                st[j, c, x + 1, 0:TOP, :] = rim
                st[j, c, x + 1, TOP + rows : 2 * TOP + rows, :] = rim
            kc[j, x + 1, 0:TOP, :] = rim
            kc[j, x + 1, TOP + rows : 2 * TOP + rows, :] = rim
            for c, field in enumerate([scaled, *species, cd]):
                lo, hi = field[0:1], field[rows - 1 : rows]
                pa[x, c : c + 1, part] = jnp.where(even_y, hi, lo)
                pb[x, c : c + 1, part] = jnp.where(even_y, lo, hi)
            weight = cd * m
            sums = halve([weight * head] + [v * m for v in species] + [m])
            place = pl.ds(x * rows, rows)
            for c in range(4):
                half[j, c, place, :] = sums[c]
            whalf[j, 0, place, :] = jnp.where(low, weight + turn(weight, 64), 0.0)
            for c in range(1, 4):
                whalf[j, c, place, :] = jnp.zeros_like(weight)
        return carry

    lax.fori_loop(0, nx, plane, 0)
    total = pipe_sums(half, hot)
    total_w = pipe_sums(whalf, hot)
    small = obs[:, 0, :]
    wide = jnp.concatenate([small] * (n_pipes // small.shape[1]), axis=1)
    place = lax.broadcasted_iota(jnp.int32, wide.shape, 1) // small.shape[1]
    mine = jnp.where(place == gy, wide, 0.0)
    second = jnp.concatenate([mine, total_w[:1]], axis=0)
    for dst in (pa, pb):
        dst[nx] = total
        dst[nx + 1] = second


def first(h, sp, cond, cap, mask, bp, obs):
    nx, rows, depth = h.shape
    chans = sp.shape[0] + 1
    n_pipes = 256
    shape = lambda *dims: jax.ShapeDtypeStruct(dims, F32)
    return pl.pallas_call(
        functools.partial(first_kernel, nx, rows, chans),
        in_specs=[HB] * 5 + [VM] * 2,
        out_specs=[VM] * 5,
        out_shape=[
            shape(2, chans, nx + 2, rows + 2 * TOP, 128),
            shape(2, nx + 2, rows + 2 * TOP, 128),
            shape(nx + 2, 8, n_pipes),
            shape(nx + 2, 8, n_pipes),
            jax.ShapeDtypeStruct((2, nx * rows, n_pipes), BF16),
        ],
        scratch_shapes=[
            pltpu.VMEM((2, 4, nx * rows, 128), F32),
            pltpu.VMEM((2, 4, nx * rows, 128), F32),
            pltpu.VMEM((nx, rows, depth), F32),
            pltpu.VMEM((nx, rows, depth), F32),
            pltpu.VMEM((nx, rows, depth), jnp.int32),
            pltpu.SemaphoreType.DMA((nx // STEP, 7)),
        ],
        compiler_params=pltpu.CompilerParams(vmem_limit_bytes=VLIM),
        cost_estimate=pl.CostEstimate(flops=10**7, bytes_accessed=8 * 10**6, transcendentals=0),
    )(h, sp, cond, cap, mask, bp, obs)


def inner_kernel(nx, rows, chans, diffusion, coupling, react, st, kc, h, rate, mat, out):
    nsp = chans - 1
    both = range(2)
    lane = lax.broadcasted_iota(jnp.int32, (RB, 128), 1)
    first_lane, last_lane = lane == 0, lane == 127

    def updown(pair):
        left = [turn(v, -1) for v in pair]
        right = [turn(v, 1) for v in pair]
        up = [jnp.where(first_lane, 0.0, left[0]), jnp.where(first_lane, left[0], left[1])]
        down = [jnp.where(last_lane, right[1], right[0]), jnp.where(last_lane, 0.0, right[1])]
        return up, down

    def plane(x, carry):
        for r in range(0, rows, RB):
            at = TOP + r
            body = slice(r, r + RB)

            def sides(ref, *lead):
                near = [
                    [
                        ref[(j, *lead, x, slice(at, at + RB))],
                        ref[(j, *lead, x + 2, slice(at, at + RB))],
                        ref[(j, *lead, x + 1, slice(at - 1, at - 1 + RB))],
                        ref[(j, *lead, x + 1, slice(at + 1, at + 1 + RB))],
                    ]
                    for j in both
                ]
                return [ref[(j, *lead, x + 1, slice(at, at + RB))] for j in both], near

            rt = [time_step * rate[x, body, LANES[j]] for j in both]
            mt = [mat[x, body, LANES[j]] for j in both]
            odd = [v % 2 == 1 for v in mt]
            high = [v >= 2 for v in mt]

            c_mid, c_near = sides(kc)
            s_mid, s_near = sides(st, 0)
            c_up, c_down = updown(c_mid)
            s_up, s_down = updown(s_mid)
            flow = []
            for j in both:
                acc = None
                near_c = c_near[j] + [c_up[j], c_down[j]]
                near_s = s_near[j] + [s_up[j], s_down[j]]
                for oc, os in zip(near_c, near_s):
                    term = (c_mid[j] + oc) * (os - s_mid[j])
                    acc = term if acc is None else acc + term
                flow.append(0.5 * acc)
            mids = []
            outs = [[None] * chans for _ in both]
            for c in range(nsp):
                mid, near = sides(st, c + 1)
                up, down = updown(mid)
                kd = time_step * diffusion[c]
                mids.append(mid)
                for j in both:
                    n4 = (near[j][0] + near[j][1]) + (near[j][2] + near[j][3])
                    n6 = n4 + (up[j] + down[j])
                    outs[j][c + 1] = mid[j] + kd * (n6 - 6.0 * mid[j])
            for j in both:
                source = None
                for c in range(nsp):
                    term = coupling[c] * mids[c][j]
                    source = term if source is None else source + term
                head = h[j, x, body] if len(h.shape) == 4 else h[x, body, LANES[j]]
                out[j, 0, x, body, :] = head + flow[j] + rt[j] * source
            for s in range(nsp):
                acc = [None, None]
                for t in range(nsp):
                    r0, r1, r2, r3 = (react[i, t, s] for i in range(4))
                    for j in both:
                        w = jnp.where(
                            high[j], jnp.where(odd[j], r3, r2), jnp.where(odd[j], r1, r0)
                        )
                        term = w * mids[t][j]
                        acc[j] = term if acc[j] is None else acc[j] + term
                for j in both:
                    out[j, s + 1, x, body, :] = outs[j][s + 1] - rt[j] * acc[j]
        return carry

    lax.fori_loop(0, nx, plane, 0)


def inner(diffusion, coupling, react, st, kc, h, rate, mat):
    nx, rows, depth = rate.shape
    chans = st.shape[1]
    return pl.pallas_call(
        functools.partial(inner_kernel, nx, rows, chans),
        in_specs=[SM] * 3 + [VM] * 5,
        out_specs=VM,
        out_shape=jax.ShapeDtypeStruct((2, chans, nx, rows, 128), F32),
        compiler_params=pltpu.CompilerParams(vmem_limit_bytes=VLIM),
        cost_estimate=pl.CostEstimate(flops=6 * 10**7, bytes_accessed=10**7, transcendentals=0),
    )(diffusion, coupling, react, st, kc, h, rate, mat)


def close_kernel(k, last, nx, rows, chans, *refs):
    refs = list(refs)
    take = lambda n: [refs.pop(0) for _ in range(n)]
    (diffusion,) = take(1)
    sums = take(k + 1)
    hot, inn, st, kc, cap, mask = take(6)
    xr1, xr2, ya, yb = take(4)
    cx1, cx2, cya, cyb = (xr1, xr2, ya, yb) if k == 0 else take(4)
    if last:
        oh, osp = take(2)
    else:
        oh, ost, px1, px2, pa, pb = take(6)
    ansb, half, xh = take(3)
    if last:
        th, tsp, sem = take(3)

    n_pipes = 256
    nsp = chans - 1
    even_x, even_y, gy = edge_flags()
    last_y = lax.axis_size("gy") - 1

    t0 = sums[0]
    root = jnp.sqrt(t0[0, 7:8, :] + 1.0)
    observed = t0[1]
    row = lax.broadcasted_iota(jnp.int32, (8, n_pipes), 0)
    weight = drain_gain * jnp.where(row == 0, t0[1, 7:8, :], t0[0, 7:8, :])
    answer = jnp.tanh(observed - t0[0] / root)
    for later in sums[1:]:
        answer = jnp.tanh(observed - (later[0] + answer * weight) / root)
    answer = drain_gain * answer
    tall = jnp.transpose(jnp.concatenate([answer, jnp.zeros((120, n_pipes), F32)], axis=0))
    pieces = jnp.concatenate(split(tall, 2), axis=1)
    part_of = lax.broadcasted_iota(jnp.int32, (256, 256), 1) // 128
    chan_of = lax.broadcasted_iota(jnp.int32, (256, 256), 0) % 128
    for j in range(2):
        picked = jnp.dot(hot[j], pieces, preferred_element_type=F32).astype(BF16)
        for c in range(0, chans, 2):
            spread = (part_of + c == chan_of).astype(BF16)
            wide = jnp.dot(picked, spread, preferred_element_type=F32)
            ansb[j, c] = wide[:, :128]
            if c + 1 < chans:
                ansb[j, c + 1] = wide[:, 128:]

    a_lo = jnp.where(even_y, 0.0, 1.0)
    b_lo = jnp.where(even_y & (gy > 0), 1.0, 0.0)
    a_hi = jnp.where(even_y, 1.0, 0.0)
    b_hi = jnp.where(even_y | (gy == last_y), 0.0, 1.0)
    row = lax.broadcasted_iota(jnp.int32, (8, 128), 0)
    top, bottom = row == 0, row == 7
    gains = jnp.zeros((8, 128), F32)
    for c in range(nsp):
        gains = jnp.where(row == c + 1, time_step * diffusion[c], gains)
    rim = jnp.zeros((TOP, 128), F32)
    if not last:
        for c in range(chans):
            clear_rim(ost, nx, rows, c)

    def pull(c_mid, s_mid, c_far, s_far):
        return 0.5 * ((c_mid + c_far) * s_far - c_far * s_mid)

    def keep(n, near, cnear):
        for c in range(chans):
            xh[n, c] = near[c]
        xh[n, chans] = cnear[chans]

    @pl.when(even_x)
    def _():
        keep(0, xr2, cx2)
        keep(1, xr1, cx1)

    @pl.when(jnp.logical_not(even_x))
    def _():
        keep(0, xr1, cx1)
        keep(1, xr2, cx2)

    def work(x, rim_at):
        for j, part in enumerate(LANES):
            def rims_of(ra, rb, wa, wb):
                return ra[x, :, part] * wa + rb[x, :, part] * wb

            m = mask[x, :, part].astype(F32)
            c_all = kc[j, x + 1, TOP : TOP + rows, :]
            add = []
            for at, wa, wb in ((0, a_lo, b_lo), (rows - 1, a_hi, b_hi)):
                far = rims_of(ya, yb, wa, wb)
                c_far = far if k == 0 else rims_of(cya, cyb, wa, wb)
                c_far = c_far[chans : chans + 1]
                s_mid = st[j, 0, x + 1, TOP + at : TOP + at + 1, :]
                head = pull(kc[j, x + 1, TOP + at : TOP + at + 1, :], s_mid, c_far, far[0:1])
                add.append((head, gains * far))
            values = []
            for c in range(chans):
                v = inn[j, c, x]
                lo, hi = ((a[0] if c == 0 else a[1][c : c + 1]) for a in add)
                v = jnp.concatenate(
                    [
                        v[:8] + jnp.where(top, lo, 0.0),
                        v[8 : rows - 8],
                        v[rows - 8 :] + jnp.where(bottom, hi, 0.0),
                    ],
                    axis=0,
                )
                if rim_at is not None:
                    far = xh[rim_at, c, :, part]
                    if c == 0:
                        s_all = st[j, 0, x + 1, TOP : TOP + rows, :]
                        v = v + pull(c_all, s_all, xh[rim_at, chans, :, part], far)
                    else:
                        v = v + time_step * diffusion[c - 1] * far
                values.append(v)
            if not last:
                drained = [v * m for v in values]
                drained[0] = drained[0] * c_all
                drained.append(jnp.zeros_like(m))
                for c, v in enumerate(halve(drained)):
                    half[j, c, pl.ds(x * rows, rows), :] = v
            for c, v in enumerate(values):
                v = v + m * ansb[j, c, pl.ds(x * rows, rows), :]
                if last:
                    if c == 0:
                        th[x, :, part] = v
                    else:
                        tsp[c - 1, x, :, part] = v
                    continue
                if c == 0:
                    oh[j, x] = v
                    v = time_step * v / cap[x, :, part]
                ost[j, c, x + 1, TOP : TOP + rows, :] = v
                ost[j, c, x + 1, 0:TOP, :] = rim
                ost[j, c, x + 1, TOP + rows : 2 * TOP + rows, :] = rim
                lo, hi = v[0:1], v[rows - 1 : rows]
                pa[x, c : c + 1, part] = jnp.where(even_y, hi, lo)
                pb[x, c : c + 1, part] = jnp.where(even_y, lo, hi)

    def result(g):
        at = pl.ds(g * STEP, STEP)
        pairs = [(th.at[at], oh.at[at]), (tsp.at[:, at], osp.at[:, at])]
        return [pltpu.make_async_copy(a, b, sem.at[g, n]) for n, (a, b) in enumerate(pairs)]

    def planes(i, carry):
        x = 2 * i
        work(x - 1, None)
        if last:

            @pl.when(x % STEP == 0)
            def _():
                for copy in result(x // STEP - 1):
                    copy.start()

        work(x, None)
        return carry

    def rim_plane(n, carry):
        work(n * (nx - 1), n)
        return carry

    lax.fori_loop(0, 2, rim_plane, 0)
    lax.fori_loop(1, nx // 2, planes, 0)
    if not last:

        def send(dst, x):
            for c in range(chans):
                for j, part in enumerate(LANES):
                    dst[c, :, part] = ost[j, c, x + 1, TOP : TOP + rows, :]

        @pl.when(even_x)
        def _():
            send(px1, nx - 1)
            send(px2, 0)

        @pl.when(jnp.logical_not(even_x))
        def _():
            send(px1, 0)
            send(px2, nx - 1)

        total = pipe_sums(half, hot)
        pa[nx] = total
        pb[nx] = total
    else:
        for copy in result(nx // STEP - 1):
            copy.start()
        for g in range(nx // STEP):
            for copy in result(g):
                copy.wait()


def close(k, diffusion, sums, hot, inn, st, kc, cap, mask, near, near0):
    last = k == ITERS - 1
    nx, rows, depth = cap.shape
    chans = st.shape[1]
    n_pipes = 256
    args = [diffusion, *sums, hot, inn, st, kc, cap, mask, *near]
    if k > 0:
        args += near0
    shape = lambda *dims: jax.ShapeDtypeStruct(dims, F32)
    scratch = [
        pltpu.VMEM((2, chans, nx * rows, 128), F32),
        pltpu.VMEM((2, 4, nx * rows, 128), F32),
        pltpu.VMEM((2, chans + 1, rows, depth), F32),
    ]
    if last:
        shapes = [shape(nx, rows, depth), shape(chans - 1, nx, rows, depth)]
        out_specs = [HB] * 2
        scratch += [
            pltpu.VMEM((nx, rows, depth), F32),
            pltpu.VMEM((chans - 1, nx, rows, depth), F32),
            pltpu.SemaphoreType.DMA((nx // STEP, 2)),
        ]
    else:
        shapes = [shape(2, nx, rows, 128), shape(*st.shape)]
        shapes += [shape(chans, rows, depth)] * 2 + [shape(nx + 1, 8, n_pipes)] * 2
        out_specs = [VM] * 6
    return pl.pallas_call(
        functools.partial(close_kernel, k, last, nx, rows, chans),
        in_specs=[SM] + [VM] * (len(args) - 1),
        out_specs=out_specs,
        out_shape=shapes,
        scratch_shapes=scratch,
        compiler_params=pltpu.CompilerParams(vmem_limit_bytes=VLIM),
        cost_estimate=pl.CostEstimate(flops=2 * 10**7, bytes_accessed=10**7, transcendentals=0),
    )(*args)


def swap(x, axis, first_low):
    count = lax.axis_size(axis)
    pairs = []
    for low in range(first_low, count - 1, 2):
        pairs += [(low, low + 1), (low + 1, low)]
    return lax.ppermute(x, axis, pairs)


def beside_x(px1, px2):
    return [swap(px1, "gx", 0), swap(px2, "gx", 1)]


def beside_y(pa, pb, nx):
    count = lax.axis_size("gy")
    ya = swap(pa, "gy", 0)
    pair_sum = pa[nx:] + ya[nx:]
    pb = lax.dynamic_update_slice(pb, pair_sum, (nx, 0, 0))
    ring = []
    for low in range(1, count, 2):
        other = (low + 1) % count
        ring += [(low, other), (other, low)]
    yb = lax.ppermute(pb, "gy", ring)
    four = pair_sum + yb[nx:]
    far = lax.ppermute(four, "gy", [(i, (i + count // 2) % count) for i in range(count)])
    return [ya, yb], four + far


def body(
    adj_head,
    adj_species,
    cond,
    capacity,
    rate,
    diffusion,
    coupling,
    react,
    material,
    drain_mask,
    block_pipe,
    pipe_obs,
):
    nx = adj_head.shape[0]
    packs = edges(adj_head, adj_species, cond, capacity)
    near_x = beside_x(*packs)
    block_pipe, _ = lax.optimization_barrier((block_pipe, packs))
    st, kc, pa, pb, hot = first(
        adj_head, adj_species, cond, capacity, drain_mask, block_pipe, pipe_obs
    )
    h = adj_head
    near0 = None
    sums = []
    for k in range(ITERS):
        near_y, total = beside_y(pa, pb, nx)
        near = near_x + near_y
        near0 = near if k == 0 else near0
        sums.append(total)
        inn = inner(diffusion, coupling, react, st, kc, h, rate, material)
        out = close(k, diffusion, sums, hot, inn, st, kc, capacity, drain_mask, near, near0)
        if k < ITERS - 1:
            h, st, px1, px2, pa, pb = out
            near_x = beside_x(px1, px2)
    return tuple(out)


def solution(mesh):
    return jax.shard_map(
        body,
        mesh=mesh,
        in_specs=(
            P("gx", "gy", None),
            P(None, "gx", "gy", None),
            P("gx", "gy", None),
            P("gx", "gy", None),
            P("gx", "gy", None),
            P(),
            P(),
            P(),
            P("gx", "gy", None),
            P("gx", "gy", None),
            P("gx", "gy", None),
            P(None, "gx", "gy"),
        ),
        out_specs=(P("gx", "gy", None), P(None, "gx", "gy", None)),
        check_vma=False,
    )
```

profile of v0, /device:TPU:6, one launch (start us, length us, event | category | flops | bytes accessed | tf_op | source)
XLA Modules:
  0.0 82.5 jit_solution(18209799160433948011)
XLA Ops:
  0.6 1.1 %dynamic-slice_bitcast_fusion = (f32[6,32,256]{2,1,0:T(8,128)S(1)}, f32[6,32,256]{2,1,0:T(8,128)S(1)}) fusion(f32[6,16,32,256]{3,2,1,0:T(8,128)} %sp.1, s32[]{:T(128)S(6)} %select_n.24, s32[]{:T(128)S(6)} %select_n.23), kind=kLoop, calls=%fused_computation.2 | loop fusion | bytes 786440 | tf_op jit(solution)/shard_map/squeeze | solution.py:111
  1.7 0.0 copy-start.12
  1.7 0.0 copy-start.4
  1.7 0.0 copy-start.5
  1.7 0.0 copy-start.9
  1.8 0.0 copy-start.10
  1.8 0.9 %dynamic-slice_divide_fusion = (f32[1,32,256]{2,1,0:T(8,128)S(1)}, f32[1,32,256]{2,1,0:T(8,128)S(1)}, f32[1,32,256]{2,1,0:T(8,128)S(1)}, f32[1,32,256]{2,1,0:T(8,128)S(1)}) fusion(f32[16,32,256]{2,1,0:T(8,128)} %refs_8_.3, s32[]{:T(128)S(6)} %select_n.24, f32[16,32,256]{2,1,0:T(8,128)} %h.3, s32[]{:T(128)S(6)} %select_n.23, f32[16,32,256]{2,1,0:T(8,128)} %cond.1), kind=kLoop, calls=%fused_computation.4 | loop fusion | flops 32768 | bytes 327688 | tf_op jit(solution)/shard_map/div | solution.py:110
  2.8 0.9 %copy.14.bp = s32[16,32,2]{2,1,0:T(8,128)S(1)} copy(s32[16,32,2]{1,2,0:T(2,128)} %param.22) | data formatting | bytes 8192 | tf_op jit(solution)/shard_map/optimization_barrier | solution.py:591
  3.7 0.0 copy-start
  3.7 1.0 %copy-done = f32[16,32,256]{2,1,0:T(8,128)S(1)} copy-done((f32[16,32,256]{2,1,0:T(8,128)S(1)}, f32[16,32,256]{2,1,0:T(8,128)}, u32[]{:S(2)}) %copy-start) | copy-done | bytes 524312
  4.7 0.0 copy-start.2
  4.7 1.0 %copy-done.2 = s32[16,32,256]{2,1,0:T(8,128)S(1)} copy-done((s32[16,32,256]{2,1,0:T(8,128)S(1)}, s32[16,32,256]{2,1,0:T(8,128)}, u32[]{:S(2)}) %copy-start.2) | copy-done | bytes 524312
  5.7 0.0 copy-start.6
  5.7 1.9 %copy-done.6 = f32[6,16,32,256]{3,2,1,0:T(8,128)S(1)} copy-done((f32[6,16,32,256]{3,2,1,0:T(8,128)S(1)}, f32[6,16,32,256]{3,2,1,0:T(8,128)}, u32[]{:S(2)}) %copy-start.6) | copy-done | bytes 3145752
  7.6 0.0 copy-start.7
  7.6 1.0 %copy-done.7 = f32[16,32,256]{2,1,0:T(8,128)S(1)} copy-done((f32[16,32,256]{2,1,0:T(8,128)S(1)}, f32[16,32,256]{2,1,0:T(8,128)}, u32[]{:S(2)}) %copy-start.7) | copy-done | bytes 524312
  8.7 0.0 copy-start.8
  8.7 1.0 %copy-done.8 = f32[16,32,256]{2,1,0:T(8,128)S(1)} copy-done((f32[16,32,256]{2,1,0:T(8,128)S(1)}, f32[16,32,256]{2,1,0:T(8,128)}, u32[]{:S(2)}) %copy-start.8) | copy-done | bytes 524312
  9.7 0.0 copy-start.11
  9.7 0.7 copy-done.11
  10.4 7.3 %shard_map.131 = (f32[2,7,18,48,128]{4,3,2,1,0:T(8,128)S(1)}, f32[2,18,48,128]{3,2,1,0:T(8,128)S(1)}, f32[18,8,256]{2,1,0:T(8,128)S(1)}, f32[18,8,256]{2,1,0:T(8,128)S(1)}, bf16[2,512,256]{2,1,0:T(8,128)(2,1)S(1)}) custom-call(f32[16,32,256]{2,1,0:T(8,128)S(1)} %copy-done.7, f32[6,16,32,256]{3,2,1,0:T(8,128)S(1)} %copy-done.6, f32[16,32,256]{2,1,0:T(8,128)S(1)} %copy-done.8, ...), custom_call_target="tpu_custom_call" | custom-call | flops 10000000 | bytes 8000000 | tf_op jit(solution)/shard_map/pallas_call | solution.py:204
  17.7 0.1 collective-permute-start
  17.8 1.4 %collective-permute-done.refs_10_.refs_15_.refs_16_ = f32[18,8,256]{2,1,0:T(8,128)S(1)} collective-permute-done((f32[18,8,256]{2,1,0:T(8,128)S(1)}, f32[18,8,256]{2,1,0:T(8,128)S(1)}, u32[]{:S(2)}, u32[]{:S(2)}) %collective-permute-start) | collective-permute-done | bytes 147488 | tf_op jit(solution)/shard_map/ppermute | solution.py:552
  19.2 3.8 %collective-permute-start.1 = (f32[18,8,256]{2,1,0:T(8,128)S(1)}, f32[18,8,256]{2,1,0:T(8,128)S(1)}, u32[]{:S(2)}, u32[]{:S(2)}) collective-permute-start(f32[18,8,256]{2,1,0:T(8,128)S(1)} %fusion), channel_id=1, source_target_pairs={{1,2},{2,1},{3,4},{4,3},{5,6},{6,5},{7,0},{0,7},{9,10},{10,9},{11,... | collective-permute-start | bytes 442376 | tf_op jit(solution)/shard_map/ppermute | solution.py:568
  23.0 1.6 %collective-permute-start.3 = (f32[8,32,256]{2,1,0:T(8,128)S(1)}, f32[8,32,256]{2,1,0:T(8,128)S(1)}, u32[]{:S(2)}, u32[]{:S(2)}) collective-permute-start(f32[8,32,256]{2,1,0:T(8,128)S(1)} %pad_maximum_fusion), channel_id=1, source_target_pairs={{0,8},{8,0},{16,24},{24,16},{32,40},{40,32},{48,56},{56,48},{64,72... | collective-permute-start | bytes 786440 | tf_op jit(solution)/shard_map/ppermute | solution.py:552
  24.6 4.3 %collective-permute-start.4 = (f32[8,32,256]{2,1,0:T(8,128)S(1)}, f32[8,32,256]{2,1,0:T(8,128)S(1)}, u32[]{:S(2)}, u32[]{:S(2)}) collective-permute-start(f32[8,32,256]{2,1,0:T(8,128)S(1)} %pad_maximum_fusion.1), channel_id=1, source_target_pairs={{8,16},{16,8},{24,32},{32,24},{40,48},{48,40},{56,64},{64,56},{72,... | collective-permute-start | bytes 786440 | tf_op jit(solution)/shard_map/ppermute | solution.py:552
  28.9 0.0 collective-permute-done.1.refs_11_.refs_16_.refs_17_
  28.9 0.3 collective-permute-start.2
  29.2 0.0 copy-done.12
  29.2 0.0 copy-done.4
  29.2 0.0 copy-done.5
  29.2 0.0 copy-done.9
  29.2 0.0 copy-done.10
  29.2 7.3 %shard_map.132.refs_3_ = f32[2,7,16,32,128]{4,3,2,1,0:T(8,128)S(1)} custom-call(f32[6]{0:T(128)S(1)} %copy-done.9, f32[6]{0:T(128)S(1)} %copy-done.10, f32[4,6,6]{2,1,0:T(8,128)S(1)} %copy.15.react, f32[2,7,18,48,128]{4,3,2,1,0:T(8,128)S(1)} %get-tuple-element.24.st.refs_4_, f32[2,18,48,128]{3,2,1,0:T(8,128)S(1)} %get-tuple-element.25.kc.refs_5_.refs_6_.refs_7_, ...), custom_call_target="tpu_custom_call" | custom-call | flops 60000000 | bytes 10000000 | tf_op jit(solution)/shard_map/pallas_call | solution.py:314
  36.5 0.0 collective-permute-done.2
  36.6 0.0 collective-permute-done.3.refs_8_.refs_13_.refs_14_
  36.6 0.0 collective-permute-done.4.refs_9_.refs_14_.refs_15_
  36.6 4.8 %shard_map.133 = (f32[2,16,32,128]{3,2,1,0:T(8,128)S(1)}, f32[2,7,18,48,128]{4,3,2,1,0:T(8,128)S(1)}, f32[7,32,256]{2,1,0:T(8,128)S(1)}, f32[7,32,256]{2,1,0:T(8...) custom-call(f32[6]{0:T(128)S(1)} %copy-done.9, f32[2,8,256]{2,1,0:T(8,128)S(1)} %add.42.refs_1_, ...), custom_call_target="tpu_custom_call" | custom-call | flops 20000000 | bytes 10000000 | tf_op jit(solution)/shard_map/pallas_call | solution.py:536
  41.4 0.8 %collective-permute-start.5 = (f32[17,8,256]{2,1,0:T(8,128)S(1)}, f32[17,8,256]{2,1,0:T(8,128)S(1)}, u32[]{:S(2)}, u32[]{:S(2)}) collective-permute-start(f32[17,8,256]{2,1,0:T(8,128)S(1)} %get-tuple-element.26), channel_id=1, source_target_pairs={{0,1},{1,0},{2,3},{3,2},{4,5},{5,4},{6,7},{7,6},{8,9},{9,8},{10,11... | collective-permute-start | bytes 417800 | tf_op jit(solution)/shard_map/ppermute | solution.py:552
  42.2 1.0 %collective-permute-done.5.refs_11_ = f32[17,8,256]{2,1,0:T(8,128)S(1)} collective-permute-done((f32[17,8,256]{2,1,0:T(8,128)S(1)}, f32[17,8,256]{2,1,0:T(8,128)S(1)}, u32[]{:S(2)}, u32[]{:S(2)}) %collective-permute-start.5) | collective-permute-done | bytes 139296 | tf_op jit(solution)/shard_map/ppermute | solution.py:552
  43.2 1.0 %collective-permute-start.6 = (f32[17,8,256]{2,1,0:T(8,128)S(1)}, f32[17,8,256]{2,1,0:T(8,128)S(1)}, u32[]{:S(2)}, u32[]{:S(2)}) collective-permute-start(f32[17,8,256]{2,1,0:T(8,128)S(1)} %constant_dynamic-update-slice_fusion.1), channel_id=1, source_target_pairs={{1,2},{2,1},{3,4},{4,3},{5,6},{6,5},{7,0},{0,7},{9,10},{10,9},{11,... | collective-permute-start | bytes 417800 | tf_op jit(solution)/shard_map/ppermute | solution.py:568
  44.2 0.4 collective-permute-start.8
  44.6 3.7 %collective-permute-start.9 = (f32[7,32,256]{2,1,0:T(8,128)S(1)}, f32[7,32,256]{2,1,0:T(8,128)S(1)}, u32[]{:S(2)}, u32[]{:S(2)}) collective-permute-start(f32[7,32,256]{2,1,0:T(8,128)S(1)} %get-tuple-element.31), channel_id=1, source_target_pairs={{8,16},{16,8},{24,32},{32,24},{40,48},{48,40},{56,64},{64,56},{72,... | collective-permute-start | bytes 688136 | tf_op jit(solution)/shard_map/ppermute | solution.py:552
  48.3 0.6 collective-permute-done.6.refs_12_
  48.9 2.1 %collective-permute-start.7 = (f32[1,8,256]{2,1,0:T(8,128)S(1)}, f32[1,8,256]{2,1,0:T(8,128)S(1)}, u32[]{:S(2)}, u32[]{:S(2)}) collective-permute-start(f32[1,8,256]{2,1,0:T(8,128)S(1)} %slice_add_fusion.4), channel_id=1, source_target_pairs={{0,4},{1,5},{2,6},{3,7},{4,0},{5,1},{6,2},{7,3},{8,12},{9,13},{10,... | collective-permute-start | bytes 24584 | tf_op jit(solution)/shard_map/ppermute | solution.py:570
  51.0 7.3 %shard_map.134.refs_4_ = f32[2,7,16,32,128]{4,3,2,1,0:T(8,128)S(1)} custom-call(f32[6]{0:T(128)S(1)} %copy-done.9, f32[6]{0:T(128)S(1)} %copy-done.10, f32[4,6,6]{2,1,0:T(8,128)S(1)} %copy.15.react, f32[2,7,18,48,128]{4,3,2,1,0:T(8,128)S(1)} %get-tuple-element.28.st.refs_5_, f32[2,18,48,128]{3,2,1,0:T(8,128)S(1)} %get-tuple-element.25.kc.refs_5_.refs_6_.refs_7_, ...), custom_call_target="tpu_custom_call" | custom-call | flops 60000000 | bytes 10000000 | tf_op jit(solution)/shard_map/pallas_call | solution.py:314
  58.3 0.0 collective-permute-done.7
  58.3 0.0 collective-permute-done.8.refs_9_
  58.3 0.0 collective-permute-done.9.refs_10_
  58.4 4.8 %shard_map.135 = (f32[2,16,32,128]{3,2,1,0:T(8,128)S(1)}, f32[2,7,18,48,128]{4,3,2,1,0:T(8,128)S(1)}, f32[7,32,256]{2,1,0:T(8,128)S(1)}, f32[7,32,256]{2,1,0:T(8...) custom-call(f32[6]{0:T(128)S(1)} %copy-done.9, f32[2,8,256]{2,1,0:T(8,128)S(1)} %add.42.refs_1_, ...), custom_call_target="tpu_custom_call" | custom-call | flops 20000000 | bytes 10000000 | tf_op jit(solution)/shard_map/pallas_call | solution.py:536
  63.1 0.0 collective-permute-start.10
  63.2 1.4 %collective-permute-done.10.refs_12_ = f32[17,8,256]{2,1,0:T(8,128)S(1)} collective-permute-done((f32[17,8,256]{2,1,0:T(8,128)S(1)}, f32[17,8,256]{2,1,0:T(8,128)S(1)}, u32[]{:S(2)}, u32[]{:S(2)}) %collective-permute-start.10) | collective-permute-done | bytes 139296 | tf_op jit(solution)/shard_map/ppermute | solution.py:552
  64.5 0.6 collective-permute-start.11
  65.1 0.3 collective-permute-start.13
  65.5 4.2 %collective-permute-start.14 = (f32[7,32,256]{2,1,0:T(8,128)S(1)}, f32[7,32,256]{2,1,0:T(8,128)S(1)}, u32[]{:S(2)}, u32[]{:S(2)}) collective-permute-start(f32[7,32,256]{2,1,0:T(8,128)S(1)} %get-tuple-element.37), channel_id=1, source_target_pairs={{8,16},{16,8},{24,32},{32,24},{40,48},{48,40},{56,64},{64,56},{72,... | collective-permute-start | bytes 688136 | tf_op jit(solution)/shard_map/ppermute | solution.py:552
  69.7 0.5 collective-permute-done.11.refs_13_
  70.2 1.0 %collective-permute-start.12 = (f32[1,8,256]{2,1,0:T(8,128)S(1)}, f32[1,8,256]{2,1,0:T(8,128)S(1)}, u32[]{:S(2)}, u32[]{:S(2)}) collective-permute-start(f32[1,8,256]{2,1,0:T(8,128)S(1)} %slice_add_fusion.2), channel_id=1, source_target_pairs={{0,4},{1,5},{2,6},{3,7},{4,0},{5,1},{6,2},{7,3},{8,12},{9,13},{10,... | collective-permute-start | bytes 24584 | tf_op jit(solution)/shard_map/ppermute | solution.py:570
  71.3 7.3 %shard_map.136.refs_5_ = f32[2,7,16,32,128]{4,3,2,1,0:T(8,128)S(1)} custom-call(f32[6]{0:T(128)S(1)} %copy-done.9, f32[6]{0:T(128)S(1)} %copy-done.10, f32[4,6,6]{2,1,0:T(8,128)S(1)} %copy.15.react, f32[2,7,18,48,128]{4,3,2,1,0:T(8,128)S(1)} %get-tuple-element.34.st.refs_6_, f32[2,18,48,128]{3,2,1,0:T(8,128)S(1)} %get-tuple-element.25.kc.refs_5_.refs_6_.refs_7_, ...), custom_call_target="tpu_custom_call" | custom-call | flops 60000000 | bytes 10000000 | tf_op jit(solution)/shard_map/pallas_call | solution.py:314
  78.6 0.0 collective-permute-done.12
  78.6 0.0 collective-permute-done.13.refs_10_
  78.6 0.0 collective-permute-done.14.refs_11_
  78.6 0.0 copy-done.1
  78.6 0.0 copy-done.3
  78.6 3.8 %shard_map.137 = (f32[16,32,256]{2,1,0:T(8,128)}, f32[6,16,32,256]{3,2,1,0:T(8,128)}) custom-call(f32[6]{0:T(128)S(1)} %copy-done.9, f32[2,8,256]{2,1,0:T(8,128)S(1)} %add.42.refs_1_, f32[1,8,256]{2,1,0:T(8,128)S(1)} %add.45.refs_2_, f32[1,8,256]{2,1,0:T(8,128)S(1)} %add.48.refs_3_, bf16[2,512,256]{2,1,0:T(8,128)(2,1)S(1)} %get-tuple-element.23.refs_2_.refs_3_.refs_4_, ...), custom_call_target="tpu_custom_call" | custom-call | flops 20000000 | bytes 10000000 | tf_op jit(solution)/shard_map/pallas_call | solution.py:536
  (14 shorter events, 0.1 us)
Async XLA Ops:
  1.7 27.5 %copy-start.12 = (f32[4,6,6]{2,0,1:T(4,128)S(1)}, f32[4,6,6]{2,0,1:T(4,128)}, u32[]{:S(2)}) copy-start(f32[4,6,6]{2,0,1:T(4,128)} %param.19) | copy-start | bytes 1732
  1.7 27.5 %copy-start.4 = (f32[16,32,256]{2,1,0:T(8,128)S(1)}, f32[16,32,256]{2,1,0:T(8,128)}, u32[]{:S(2)}) copy-start(f32[16,32,256]{2,1,0:T(8,128)} %rate.5) | copy-start | bytes 1572868
  1.7 27.5 %copy-start.5 = (s32[16,32,256]{2,1,0:T(8,128)S(1)}, s32[16,32,256]{2,1,0:T(8,128)}, u32[]{:S(2)}) copy-start(s32[16,32,256]{2,1,0:T(8,128)} %mat.5) | copy-start | bytes 1572868
  1.7 27.5 %copy-start.9 = (f32[6]{0:T(128)S(1)}, f32[6]{0:T(128)}, u32[]{:S(2)}) copy-start(f32[6]{0:T(128)} %refs_0_.5) | copy-start | bytes 76
  1.8 27.5 %copy-start.10 = (f32[6]{0:T(128)S(1)}, f32[6]{0:T(128)}, u32[]{:S(2)}) copy-start(f32[6]{0:T(128)} %coupling.5) | copy-start | bytes 76
  3.7 1.0 %copy-start = (f32[16,32,256]{2,1,0:T(8,128)S(1)}, f32[16,32,256]{2,1,0:T(8,128)}, u32[]{:S(2)}) copy-start(f32[16,32,256]{2,1,0:T(8,128)} %refs_8_.3) | copy-start | bytes 1572868
  4.7 1.0 %copy-start.2 = (s32[16,32,256]{2,1,0:T(8,128)S(1)}, s32[16,32,256]{2,1,0:T(8,128)}, u32[]{:S(2)}) copy-start(s32[16,32,256]{2,1,0:T(8,128)} %refs_9_.1) | copy-start | bytes 1572868
  5.7 1.9 %copy-start.6 = (f32[6,16,32,256]{3,2,1,0:T(8,128)S(1)}, f32[6,16,32,256]{3,2,1,0:T(8,128)}, u32[]{:S(2)}) copy-start(f32[6,16,32,256]{3,2,1,0:T(8,128)} %sp.1) | copy-start | bytes 9437188
  7.6 1.0 %copy-start.7 = (f32[16,32,256]{2,1,0:T(8,128)S(1)}, f32[16,32,256]{2,1,0:T(8,128)}, u32[]{:S(2)}) copy-start(f32[16,32,256]{2,1,0:T(8,128)} %h.3) | copy-start | bytes 1572868
  8.7 1.0 %copy-start.8 = (f32[16,32,256]{2,1,0:T(8,128)S(1)}, f32[16,32,256]{2,1,0:T(8,128)}, u32[]{:S(2)}) copy-start(f32[16,32,256]{2,1,0:T(8,128)} %cond.1) | copy-start | bytes 1572868
  9.7 0.7 copy-start.11
  17.7 1.5 %collective-permute-start = (f32[18,8,256]{2,1,0:T(8,128)S(1)}, f32[18,8,256]{2,1,0:T(8,128)S(1)}, u32[]{:S(2)}, u32[]{:S(2)}) collective-permute-start(f32[18,8,256]{2,1,0:T(8,128)S(1)} %get-tuple-element.21), channel_id=1, source_target_pairs={{0,1},{1,0},{2,3},{3,2},{4,5},{5,4},{6,7},{7,6},{8,9},{9,8},{10,11... | collective-permute-start | bytes 442376 | tf_op jit(solution)/shard_map/ppermute | solution.py:552
  19.2 9.7 %collective-permute-start.1 = (f32[18,8,256]{2,1,0:T(8,128)S(1)}, f32[18,8,256]{2,1,0:T(8,128)S(1)}, u32[]{:S(2)}, u32[]{:S(2)}) collective-permute-start(f32[18,8,256]{2,1,0:T(8,128)S(1)} %fusion), channel_id=1, source_target_pairs={{1,2},{2,1},{3,4},{4,3},{5,6},{6,5},{7,0},{0,7},{9,10},{10,9},{11,... | collective-permute-start | bytes 442376 | tf_op jit(solution)/shard_map/ppermute | solution.py:568
  23.0 13.6 %collective-permute-start.3 = (f32[8,32,256]{2,1,0:T(8,128)S(1)}, f32[8,32,256]{2,1,0:T(8,128)S(1)}, u32[]{:S(2)}, u32[]{:S(2)}) collective-permute-start(f32[8,32,256]{2,1,0:T(8,128)S(1)} %pad_maximum_fusion), channel_id=1, source_target_pairs={{0,8},{8,0},{16,24},{24,16},{32,40},{40,32},{48,56},{56,48},{64,72... | collective-permute-start | bytes 786440 | tf_op jit(solution)/shard_map/ppermute | solution.py:552
  24.6 12.0 %collective-permute-start.4 = (f32[8,32,256]{2,1,0:T(8,128)S(1)}, f32[8,32,256]{2,1,0:T(8,128)S(1)}, u32[]{:S(2)}, u32[]{:S(2)}) collective-permute-start(f32[8,32,256]{2,1,0:T(8,128)S(1)} %pad_maximum_fusion.1), channel_id=1, source_target_pairs={{8,16},{16,8},{24,32},{32,24},{40,48},{48,40},{56,64},{64,56},{72,... | collective-permute-start | bytes 786440 | tf_op jit(solution)/shard_map/ppermute | solution.py:552
  28.9 7.6 %collective-permute-start.2 = (f32[2,8,256]{2,1,0:T(8,128)S(1)}, f32[2,8,256]{2,1,0:T(8,128)S(1)}, u32[]{:S(2)}, u32[]{:S(2)}) collective-permute-start(f32[2,8,256]{2,1,0:T(8,128)S(1)} %slice_add_fusion), channel_id=1, source_target_pairs={{0,4},{1,5},{2,6},{3,7},{4,0},{5,1},{6,2},{7,3},{8,12},{9,13},{10,... | collective-permute-start | bytes 49160 | tf_op jit(solution)/shard_map/ppermute | solution.py:570
  41.4 1.8 %collective-permute-start.5 = (f32[17,8,256]{2,1,0:T(8,128)S(1)}, f32[17,8,256]{2,1,0:T(8,128)S(1)}, u32[]{:S(2)}, u32[]{:S(2)}) collective-permute-start(f32[17,8,256]{2,1,0:T(8,128)S(1)} %get-tuple-element.26), channel_id=1, source_target_pairs={{0,1},{1,0},{2,3},{3,2},{4,5},{5,4},{6,7},{7,6},{8,9},{9,8},{10,11... | collective-permute-start | bytes 417800 | tf_op jit(solution)/shard_map/ppermute | solution.py:552
  43.2 5.7 %collective-permute-start.6 = (f32[17,8,256]{2,1,0:T(8,128)S(1)}, f32[17,8,256]{2,1,0:T(8,128)S(1)}, u32[]{:S(2)}, u32[]{:S(2)}) collective-permute-start(f32[17,8,256]{2,1,0:T(8,128)S(1)} %constant_dynamic-update-slice_fusion.1), channel_id=1, source_target_pairs={{1,2},{2,1},{3,4},{4,3},{5,6},{6,5},{7,0},{0,7},{9,10},{10,9},{11,... | collective-permute-start | bytes 417800 | tf_op jit(solution)/shard_map/ppermute | solution.py:568
  44.2 14.2 %collective-permute-start.8 = (f32[7,32,256]{2,1,0:T(8,128)S(1)}, f32[7,32,256]{2,1,0:T(8,128)S(1)}, u32[]{:S(2)}, u32[]{:S(2)}) collective-permute-start(f32[7,32,256]{2,1,0:T(8,128)S(1)} %get-tuple-element.30), channel_id=1, source_target_pairs={{0,8},{8,0},{16,24},{24,16},{32,40},{40,32},{48,56},{56,48},{64,72... | collective-permute-start | bytes 688136 | tf_op jit(solution)/shard_map/ppermute | solution.py:552
  44.6 13.7 %collective-permute-start.9 = (f32[7,32,256]{2,1,0:T(8,128)S(1)}, f32[7,32,256]{2,1,0:T(8,128)S(1)}, u32[]{:S(2)}, u32[]{:S(2)}) collective-permute-start(f32[7,32,256]{2,1,0:T(8,128)S(1)} %get-tuple-element.31), channel_id=1, source_target_pairs={{8,16},{16,8},{24,32},{32,24},{40,48},{48,40},{56,64},{64,56},{72,... | collective-permute-start | bytes 688136 | tf_op jit(solution)/shard_map/ppermute | solution.py:552
  48.9 9.4 %collective-permute-start.7 = (f32[1,8,256]{2,1,0:T(8,128)S(1)}, f32[1,8,256]{2,1,0:T(8,128)S(1)}, u32[]{:S(2)}, u32[]{:S(2)}) collective-permute-start(f32[1,8,256]{2,1,0:T(8,128)S(1)} %slice_add_fusion.4), channel_id=1, source_target_pairs={{0,4},{1,5},{2,6},{3,7},{4,0},{5,1},{6,2},{7,3},{8,12},{9,13},{10,... | collective-permute-start | bytes 24584 | tf_op jit(solution)/shard_map/ppermute | solution.py:570
  63.1 1.4 %collective-permute-start.10 = (f32[17,8,256]{2,1,0:T(8,128)S(1)}, f32[17,8,256]{2,1,0:T(8,128)S(1)}, u32[]{:S(2)}, u32[]{:S(2)}) collective-permute-start(f32[17,8,256]{2,1,0:T(8,128)S(1)} %get-tuple-element.32), channel_id=1, source_target_pairs={{0,1},{1,0},{2,3},{3,2},{4,5},{5,4},{6,7},{7,6},{8,9},{9,8},{10,11... | collective-permute-start | bytes 417800 | tf_op jit(solution)/shard_map/ppermute | solution.py:552
  64.5 5.7 %collective-permute-start.11 = (f32[17,8,256]{2,1,0:T(8,128)S(1)}, f32[17,8,256]{2,1,0:T(8,128)S(1)}, u32[]{:S(2)}, u32[]{:S(2)}) collective-permute-start(f32[17,8,256]{2,1,0:T(8,128)S(1)} %constant_dynamic-update-slice_fusion), channel_id=1, source_target_pairs={{1,2},{2,1},{3,4},{4,3},{5,6},{6,5},{7,0},{0,7},{9,10},{10,9},{11,... | collective-permute-start | bytes 417800 | tf_op jit(solution)/shard_map/ppermute | solution.py:568
  65.1 13.4 %collective-permute-start.13 = (f32[7,32,256]{2,1,0:T(8,128)S(1)}, f32[7,32,256]{2,1,0:T(8,128)S(1)}, u32[]{:S(2)}, u32[]{:S(2)}) collective-permute-start(f32[7,32,256]{2,1,0:T(8,128)S(1)} %get-tuple-element.36), channel_id=1, source_target_pairs={{0,8},{8,0},{16,24},{24,16},{32,40},{40,32},{48,56},{56,48},{64,72... | collective-permute-start | bytes 688136 | tf_op jit(solution)/shard_map/ppermute | solution.py:552
  65.5 13.1 %collective-permute-start.14 = (f32[7,32,256]{2,1,0:T(8,128)S(1)}, f32[7,32,256]{2,1,0:T(8,128)S(1)}, u32[]{:S(2)}, u32[]{:S(2)}) collective-permute-start(f32[7,32,256]{2,1,0:T(8,128)S(1)} %get-tuple-element.37), channel_id=1, source_target_pairs={{8,16},{16,8},{24,32},{32,24},{40,48},{48,40},{56,64},{64,56},{72,... | collective-permute-start | bytes 688136 | tf_op jit(solution)/shard_map/ppermute | solution.py:552
  70.2 8.3 %collective-permute-start.12 = (f32[1,8,256]{2,1,0:T(8,128)S(1)}, f32[1,8,256]{2,1,0:T(8,128)S(1)}, u32[]{:S(2)}, u32[]{:S(2)}) collective-permute-start(f32[1,8,256]{2,1,0:T(8,128)S(1)} %slice_add_fusion.2), channel_id=1, source_target_pairs={{0,4},{1,5},{2,6},{3,7},{4,0},{5,1},{6,2},{7,3},{8,12},{9,13},{10,... | collective-permute-start | bytes 24584 | tf_op jit(solution)/shard_map/ppermute | solution.py:570
  71.3 7.3 %copy-start.1 = (f32[16,32,256]{2,1,0:T(8,128)S(1)}, f32[16,32,256]{2,1,0:T(8,128)}, u32[]{:S(2)}) copy-start(f32[16,32,256]{2,1,0:T(8,128)} %refs_8_.3) | copy-start | bytes 1572868
  71.3 7.4 %copy-start.3 = (s32[16,32,256]{2,1,0:T(8,128)S(1)}, s32[16,32,256]{2,1,0:T(8,128)}, u32[]{:S(2)}) copy-start(s32[16,32,256]{2,1,0:T(8,128)} %refs_9_.1) | copy-start | bytes 1572868
where the time goes:
time: 83 us; the launch traced here: 82.5 us
  Pallas kernels  42.6 us (51%)
  starting transfers between devices  24.3 us (29%)
  local copies, waits for them, and re-layouts  8.73 us (11%)
  waiting for transfers between devices  4.88 us (6%)
  other arithmetic  1.02 us (1%)
  between operations  0.95 us (1%)
    pallas_call x3, Pallas kernels, inner(): pl.pallas_call(functools.partial(inner_kernel, nx, rows, chans), in_specs...  21.9 us
    ppermute x9, starting transfers between devices, swap(): return lax.ppermute(x, axis, pairs)  15.5 us
    pallas_call x3, Pallas kernels, close(): pl.pallas_call(functools.partial(close_kernel, k, last, nx, rows, chans),...  13.4 us
    pallas_call x1, Pallas kernels, first(): pl.pallas_call(functools.partial(first_kernel, nx, rows, chans), in_specs...  7.33 us
    unnamed x27, local copies, waits for them, and re-layouts  6.78 us
    ppermute x3, starting transfers between devices, beside_y(): yb = lax.ppermute(pb, 'gy', ring)  5.38 us
    ppermute x9, waiting for transfers between devices, swap(): return lax.ppermute(x, axis, pairs)  3.74 us
    ppermute x3, starting transfers between devices, beside_y(): lax.ppermute(four, 'gy', [(i, (i + count // 2) % count) for i in range(co...  3.4 us
  transfers between devices with their start and end apart: 15, of which 5 were waited for; matrix products, arithmetic and copies ran while one was open for 0% of the time, Pallas kernels for 27%

commit v1 on v0

--- a/solution.py
+++ b/solution.py
@@ -22,7 +22,7 @@
 RB = 16
 
 
-VLIM = 18 * 2**20
+VLIM = 14 * 2**20
 LANES = (slice(0, 128), slice(128, 256))
 
 
@@ -35,10 +35,18 @@
     return out
 
 
-def block_onehot(bp, block, n_pipes):
-    col = bp[:, :, block : block + 1]
-    col = col.reshape(col.shape[0] * col.shape[1], 1)
-    return (col == lax.broadcasted_iota(jnp.int32, (col.shape[0], n_pipes), 1)).astype(BF16)
+def block_onehots(bp, hot):
+    nx, blocks, rows = bp.shape
+    n_pipes = hot.shape[2]
+    flat = bp[...].astype(F32).reshape(nx * blocks, rows)
+    flat = jnp.concatenate([flat, jnp.zeros((128 - nx * blocks, rows), F32)], axis=0)
+    tall = jnp.transpose(jnp.concatenate([flat, jnp.zeros((128, 128 - rows), F32)], axis=1))
+    pipe = lax.broadcasted_iota(jnp.int32, (rows, n_pipes), 1).astype(F32)
+    for x in range(nx):
+        for j in range(blocks):
+            n = x * blocks + j
+            match = tall[:rows, n : n + 1] == pipe
+            hot[j, x * rows : (x + 1) * rows, :] = match.astype(BF16)
 
 
 def turn(x, by):
@@ -101,18 +109,6 @@
     return gx % 2 == 0, gy % 2 == 0, gy
 
 
-def edges(h, sp, cond, cap):
-    nx = h.shape[0]
-    even = lax.axis_index("gx") % 2 == 0
-
-    def pack(x):
-        plane = lambda a, dim: lax.dynamic_slice_in_dim(a, x, 1, axis=dim)
-        scaled = time_step * plane(h, 0) / plane(cap, 0)
-        return jnp.concatenate([scaled, plane(sp, 1)[:, 0], plane(cond, 0)], axis=0)
-
-    return pack(jnp.where(even, nx - 1, 0)), pack(jnp.where(even, 0, nx - 1))
-
-
 def clear_rim(ref, nx, rows, *lead):
     tile = jnp.zeros((TOP, 128), F32)
     for j in range(2):
@@ -122,75 +118,79 @@
 
 
 def first_kernel(
-    nx, rows, chans, h, sp, cond, cap, mask, bp, obs, st, kc, pa, pb, hot, half, whalf, vh, vcap, vmask, sem
+    nx, rows, chans, h, sp, cond, cap, mask, bp, obs, px1, px2, pa, pb, hot,
+    half, vh, vs, vk, vcap, vmask, sem, tiny_sem, vbp, vobs
 ):
-    _, even_y, gy = edge_flags()
-    nsp = chans - 1
+    even_x, even_y, gy = edge_flags()
     n_pipes = pa.shape[2]
-    inside = pl.ds(TOP, rows)
 
     def chunk(g):
-        at, into = pl.ds(g * STEP, STEP), pl.ds(g * STEP + 1, STEP)
-        pairs = []
-        for j in range(2):
-            part = pl.ds(128 * j, 128)
-            pairs.append((sp.at[:, at, :, part], st.at[j, pl.ds(1, nsp), into, inside, :]))
-            pairs.append((cond.at[at, :, part], kc.at[j, into, inside, :]))
-        for src, dst in ((h, vh), (cap, vcap), (mask, vmask)):
+        at = pl.ds(g * STEP, STEP)
+        pairs = [(sp.at[:, at], vs.at[:, at])]
+        for src, dst in ((h, vh), (cond, vk), (cap, vcap), (mask, vmask)):
             pairs.append((src.at[at], dst.at[at]))
         return [pltpu.make_async_copy(a, b, sem.at[g, n]) for n, (a, b) in enumerate(pairs)]
 
+    tiny = [pltpu.make_async_copy(bp, vbp, tiny_sem.at[0]), pltpu.make_async_copy(obs, vobs, tiny_sem.at[1])]
+    for copy in tiny:
+        copy.start()
     for g in range(nx // STEP):
         for copy in chunk(g):
             copy.start()
-    for j in range(2):
-        hot[j] = block_onehot(bp[...], j, n_pipes)
-    for c in range(chans):
-        clear_rim(st, nx, rows, c)
-    clear_rim(kc, nx, rows)
-    rim = jnp.zeros((TOP, 128), F32)
-    low = lax.broadcasted_iota(jnp.int32, (rows, 128), 1) < 64
-
-    def plane(x, carry):
-        @pl.when(x % STEP == 0)
+    for copy in tiny:
+        copy.wait()
+    block_onehots(vbp, hot)
+
+    def planes(i, carry):
+        @pl.when(i % (STEP // 2) == 0)
         def _():
-            for copy in chunk(x // STEP):
+            for copy in chunk(i // (STEP // 2)):
                 copy.wait()
 
+        work(2 * i)
+        work(2 * i + 1)
+        return carry
+
+    def work(x):
         for j, part in enumerate(LANES):
-            cd = kc[j, x + 1, TOP : TOP + rows, :]
+            cd = vk[x, :, part]
             head = vh[x, :, part]
             m = vmask[x, :, part].astype(F32)
             scaled = time_step * head / vcap[x, :, part]
-            st[j, 0, x + 1, TOP : TOP + rows, :] = scaled
-            species = [st[j, c, x + 1, TOP : TOP + rows, :] for c in range(1, chans)]
-            for c in range(chans):
-                st[j, c, x + 1, 0:TOP, :] = rim
-                st[j, c, x + 1, TOP + rows : 2 * TOP + rows, :] = rim
-            kc[j, x + 1, 0:TOP, :] = rim
-            kc[j, x + 1, TOP + rows : 2 * TOP + rows, :] = rim
+            species = [vs[c, x, :, part] for c in range(chans - 1)]
             for c, field in enumerate([scaled, *species, cd]):
                 lo, hi = field[0:1], field[rows - 1 : rows]
                 pa[x, c : c + 1, part] = jnp.where(even_y, hi, lo)
                 pb[x, c : c + 1, part] = jnp.where(even_y, lo, hi)
-            weight = cd * m
-            sums = halve([weight * head] + [v * m for v in species] + [m])
+            sums = halve([cd * m * head] + [v * m for v in species] + [m])
             place = pl.ds(x * rows, rows)
             for c in range(4):
                 half[j, c, place, :] = sums[c]
-            whalf[j, 0, place, :] = jnp.where(low, weight + turn(weight, 64), 0.0)
-            for c in range(1, 4):
-                whalf[j, c, place, :] = jnp.zeros_like(weight)
-        return carry
-
-    lax.fori_loop(0, nx, plane, 0)
+
+    lax.fori_loop(0, nx // 2, planes, 0)
+
+    def send(dst, x):
+        dst[0] = time_step * vh[x] / vcap[x]
+        for c in range(chans - 1):
+            dst[c + 1] = vs[c, x]
+        dst[chans] = vk[x]
+
+    @pl.when(even_x)
+    def _():
+        send(px1, nx - 1)
+        send(px2, 0)
+
+    @pl.when(jnp.logical_not(even_x))
+    def _():
+        send(px1, 0)
+        send(px2, nx - 1)
+
     total = pipe_sums(half, hot)
-    total_w = pipe_sums(whalf, hot)
-    small = obs[:, 0, :]
+    small = vobs[:, 0, :]
     wide = jnp.concatenate([small] * (n_pipes // small.shape[1]), axis=1)
     place = lax.broadcasted_iota(jnp.int32, wide.shape, 1) // small.shape[1]
     mine = jnp.where(place == gy, wide, 0.0)
-    second = jnp.concatenate([mine, total_w[:1]], axis=0)
+    second = jnp.concatenate([mine, jnp.zeros((1, n_pipes), F32)], axis=0)
     for dst in (pa, pb):
         dst[nx] = total
         dst[nx + 1] = second
@@ -201,31 +201,40 @@
     chans = sp.shape[0] + 1
     n_pipes = 256
     shape = lambda *dims: jax.ShapeDtypeStruct(dims, F32)
+    field = lambda dtype: pltpu.VMEM((nx, rows, depth), dtype)
     return pl.pallas_call(
         functools.partial(first_kernel, nx, rows, chans),
-        in_specs=[HB] * 5 + [VM] * 2,
+        in_specs=[HB] * 7,
         out_specs=[VM] * 5,
         out_shape=[
-            shape(2, chans, nx + 2, rows + 2 * TOP, 128),
-            shape(2, nx + 2, rows + 2 * TOP, 128),
+            shape(chans + 1, rows, depth),
+            shape(chans + 1, rows, depth),
             shape(nx + 2, 8, n_pipes),
             shape(nx + 2, 8, n_pipes),
             jax.ShapeDtypeStruct((2, nx * rows, n_pipes), BF16),
         ],
         scratch_shapes=[
             pltpu.VMEM((2, 4, nx * rows, 128), F32),
-            pltpu.VMEM((2, 4, nx * rows, 128), F32),
-            pltpu.VMEM((nx, rows, depth), F32),
-            pltpu.VMEM((nx, rows, depth), F32),
-            pltpu.VMEM((nx, rows, depth), jnp.int32),
-            pltpu.SemaphoreType.DMA((nx // STEP, 7)),
+            field(F32),
+            pltpu.VMEM(sp.shape, F32),
+            field(F32),
+            field(F32),
+            field(jnp.int32),
+            pltpu.SemaphoreType.DMA((nx // STEP, 5)),
+            pltpu.SemaphoreType.DMA((2,)),
+            pltpu.VMEM(bp.shape, jnp.int32),
+            pltpu.VMEM(obs.shape, F32),
         ],
-        compiler_params=pltpu.CompilerParams(vmem_limit_bytes=VLIM),
+        compiler_params=pltpu.CompilerParams(vmem_limit_bytes=53 * 2**20),
         cost_estimate=pl.CostEstimate(flops=10**7, bytes_accessed=8 * 10**6, transcendentals=0),
     )(h, sp, cond, cap, mask, bp, obs)
 
 
-def inner_kernel(nx, rows, chans, diffusion, coupling, react, st, kc, h, rate, mat, out):
+def inner_kernel(fresh, nx, rows, chans, diffusion, coupling, react, rate, h, *refs):
+    if fresh:
+        mat, cap, sp, cond, coef, kc, out, st, vh, vcap, sem = refs
+    else:
+        coef, kc, st, out = refs
     nsp = chans - 1
     both = range(2)
     lane = lax.broadcasted_iota(jnp.int32, (RB, 128), 1)
@@ -238,7 +247,55 @@
         down = [jnp.where(last_lane, right[1], right[0]), jnp.where(last_lane, 0.0, right[1])]
         return up, down
 
+    def chunk(g):
+        at, into = pl.ds(g * STEP, STEP), pl.ds(g * STEP + 1, STEP)
+        inside = pl.ds(TOP, rows)
+        pairs = []
+        for j, part in enumerate((pl.ds(0, 128), pl.ds(128, 128))):
+            pairs.append((sp.at[:, at, :, part], st.at[j, pl.ds(1, nsp), into, inside, :]))
+            pairs.append((cond.at[at, :, part], kc.at[j, into, inside, :]))
+        for src, dst in ((h, vh), (cap, vcap)):
+            pairs.append((src.at[at], dst.at[at]))
+        return [pltpu.make_async_copy(a, b, sem.at[g, n]) for n, (a, b) in enumerate(pairs)]
+
+    def arrive(g):
+        for copy in chunk(g):
+            copy.wait()
+
+    def scale(x):
+        for j in both:
+            scaled = time_step * vh[x, :, LANES[j]] / vcap[x, :, LANES[j]]
+            st[j, 0, x + 1, TOP : TOP + rows, :] = scaled
+
+    if fresh:
+        for g in range(nx // STEP):
+            for copy in chunk(g):
+                copy.start()
+        for c in range(chans):
+            clear_rim(st, nx, rows, c)
+        clear_rim(kc, nx, rows)
+
+        def rims(x, carry):
+            rim = jnp.zeros((1, 128), F32)
+            for j in both:
+                for at in (slice(TOP - 1, TOP), slice(TOP + rows, TOP + rows + 1)):
+                    for c in range(chans):
+                        st[j, c, x, at, :] = rim
+                    kc[j, x, at, :] = rim
+            return carry
+
+        lax.fori_loop(1, nx + 1, rims, 0)
+        arrive(0)
+        scale(0)
+        scale(1)
+
     def plane(x, carry):
+        if fresh:
+
+            @pl.when((x % STEP == STEP - 2) & (x < nx - 2))
+            def _():
+                arrive(x // STEP + 1)
+
         for r in range(0, rows, RB):
             at = TOP + r
             body = slice(r, r + RB)
@@ -256,9 +313,10 @@
                 return [ref[(j, *lead, x + 1, slice(at, at + RB))] for j in both], near
 
             rt = [time_step * rate[x, body, LANES[j]] for j in both]
-            mt = [mat[x, body, LANES[j]] for j in both]
-            odd = [v % 2 == 1 for v in mt]
-            high = [v >= 2 for v in mt]
+            if fresh:
+                mt = [mat[x, body, LANES[j]] for j in both]
+                odd = [v % 2 == 1 for v in mt]
+                high = [v >= 2 for v in mt]
 
             c_mid, c_near = sides(kc)
             s_mid, s_near = sides(st, 0)
@@ -289,36 +347,69 @@
                 for c in range(nsp):
                     term = coupling[c] * mids[c][j]
                     source = term if source is None else source + term
-                head = h[j, x, body] if len(h.shape) == 4 else h[x, body, LANES[j]]
+                head = vh[x, body, LANES[j]] if fresh else h[j, x, body]
                 out[j, 0, x, body, :] = head + flow[j] + rt[j] * source
             for s in range(nsp):
-                acc = [None, None]
+                acc = [outs[j][s + 1] for j in both]
                 for t in range(nsp):
-                    r0, r1, r2, r3 = (react[i, t, s] for i in range(4))
+                    n = s * nsp + t
                     for j in both:
-                        w = jnp.where(
-                            high[j], jnp.where(odd[j], r3, r2), jnp.where(odd[j], r1, r0)
-                        )
-                        term = w * mids[t][j]
-                        acc[j] = term if acc[j] is None else acc[j] + term
+                        if fresh:
+                            r0, r1, r2, r3 = (react[i, t, s] for i in range(4))
+                            w = jnp.where(
+                                high[j], jnp.where(odd[j], r3, r2), jnp.where(odd[j], r1, r0)
+                            )
+                            w = w * -rt[j]
+                            coef[j, n, x, body, :] = w
+                        else:
+                            w = coef[j, n, x, body, :]
+                        acc[j] = acc[j] + w * mids[t][j]
                 for j in both:
-                    out[j, s + 1, x, body, :] = outs[j][s + 1] - rt[j] * acc[j]
+                    out[j, s + 1, x, body, :] = acc[j]
+        if fresh:
+            scale(jnp.minimum(x + 2, nx - 1))
         return carry
 
     lax.fori_loop(0, nx, plane, 0)
 
 
-def inner(diffusion, coupling, react, st, kc, h, rate, mat):
-    nx, rows, depth = rate.shape
+def inner(diffusion, coupling, react, rate, h, coef, kc, st):
+    nx, rows, _ = rate.shape
     chans = st.shape[1]
     return pl.pallas_call(
-        functools.partial(inner_kernel, nx, rows, chans),
+        functools.partial(inner_kernel, False, nx, rows, chans),
         in_specs=[SM] * 3 + [VM] * 5,
         out_specs=VM,
         out_shape=jax.ShapeDtypeStruct((2, chans, nx, rows, 128), F32),
-        compiler_params=pltpu.CompilerParams(vmem_limit_bytes=VLIM),
-        cost_estimate=pl.CostEstimate(flops=6 * 10**7, bytes_accessed=10**7, transcendentals=0),
-    )(diffusion, coupling, react, st, kc, h, rate, mat)
+        compiler_params=pltpu.CompilerParams(vmem_limit_bytes=2 * 2**20),
+        cost_estimate=pl.CostEstimate(flops=6 * 10**7, bytes_accessed=3 * 10**7, transcendentals=0),
+    )(diffusion, coupling, react, rate, h, coef, kc, st)
+
+
+def first_inner(diffusion, coupling, react, rate, h, mat, cap, sp, cond):
+    nx, rows, depth = rate.shape
+    nsp = sp.shape[0]
+    chans = nsp + 1
+    shape = lambda *dims: jax.ShapeDtypeStruct(dims, F32)
+    padded = (nx + 2, rows + 2 * TOP, 128)
+    return pl.pallas_call(
+        functools.partial(inner_kernel, True, nx, rows, chans),
+        in_specs=[SM] * 3 + [VM, HB, VM, HB, HB, HB],
+        out_specs=[VM] * 3,
+        out_shape=[
+            shape(2, nsp * nsp, nx, rows, 128),
+            shape(2, *padded),
+            shape(2, chans, nx, rows, 128),
+        ],
+        scratch_shapes=[
+            pltpu.VMEM((2, chans, *padded), F32),
+            pltpu.VMEM((nx, rows, depth), F32),
+            pltpu.VMEM((nx, rows, depth), F32),
+            pltpu.SemaphoreType.DMA((nx // STEP, 6)),
+        ],
+        compiler_params=pltpu.CompilerParams(vmem_limit_bytes=12 * 2**20),
+        cost_estimate=pl.CostEstimate(flops=6 * 10**7, bytes_accessed=3 * 10**7, transcendentals=0),
+    )(diffusion, coupling, react, rate, h, mat, cap, sp, cond)
 
 
 def close_kernel(k, last, nx, rows, chans, *refs):
@@ -326,7 +417,8 @@
     take = lambda n: [refs.pop(0) for _ in range(n)]
     (diffusion,) = take(1)
     sums = take(k + 1)
-    hot, inn, st, kc, cap, mask = take(6)
+    hot, inn, kc, cap, mask = take(5)
+    ox1, ox2, oya, oyb = take(4)
     xr1, xr2, ya, yb = take(4)
     cx1, cx2, cya, cyb = (xr1, xr2, ya, yb) if k == 0 else take(4)
     if last:
@@ -346,8 +438,9 @@
     root = jnp.sqrt(t0[0, 7:8, :] + 1.0)
     observed = t0[1]
     row = lax.broadcasted_iota(jnp.int32, (8, n_pipes), 0)
-    weight = drain_gain * jnp.where(row == 0, t0[1, 7:8, :], t0[0, 7:8, :])
     answer = jnp.tanh(observed - t0[0] / root)
+    if k > 0:
+        weight = drain_gain * jnp.where(row == 0, sums[1][0, 7:8, :], t0[0, 7:8, :])
     for later in sums[1:]:
         answer = jnp.tanh(observed - (later[0] + answer * weight) / root)
     answer = drain_gain * answer
@@ -381,20 +474,21 @@
     def pull(c_mid, s_mid, c_far, s_far):
         return 0.5 * ((c_mid + c_far) * s_far - c_far * s_mid)
 
-    def keep(n, near, cnear):
+    def keep(n, near, cnear, own):
+        xh[n, chans + 1] = own[0]
         for c in range(chans):
             xh[n, c] = near[c]
         xh[n, chans] = cnear[chans]
 
     @pl.when(even_x)
     def _():
-        keep(0, xr2, cx2)
-        keep(1, xr1, cx1)
+        keep(0, xr2, cx2, ox2)
+        keep(1, xr1, cx1, ox1)
 
     @pl.when(jnp.logical_not(even_x))
     def _():
-        keep(0, xr1, cx1)
-        keep(1, xr2, cx2)
+        keep(0, xr1, cx1, ox1)
+        keep(1, xr2, cx2, ox2)
 
     def work(x, rim_at):
         for j, part in enumerate(LANES):
@@ -408,7 +502,7 @@
                 far = rims_of(ya, yb, wa, wb)
                 c_far = far if k == 0 else rims_of(cya, cyb, wa, wb)
                 c_far = c_far[chans : chans + 1]
-                s_mid = st[j, 0, x + 1, TOP + at : TOP + at + 1, :]
+                s_mid = jnp.where(even_y == (at > 0), oya[x, 0:1, part], oyb[x, 0:1, part])
                 head = pull(kc[j, x + 1, TOP + at : TOP + at + 1, :], s_mid, c_far, far[0:1])
                 add.append((head, gains * far))
             values = []
@@ -426,15 +520,14 @@
                 if rim_at is not None:
                     far = xh[rim_at, c, :, part]
                     if c == 0:
-                        s_all = st[j, 0, x + 1, TOP : TOP + rows, :]
-                        v = v + pull(c_all, s_all, xh[rim_at, chans, :, part], far)
+                        v = v + pull(c_all, xh[rim_at, chans + 1, :, part], xh[rim_at, chans, :, part], far)
                     else:
                         v = v + time_step * diffusion[c - 1] * far
                 values.append(v)
             if not last:
                 drained = [v * m for v in values]
                 drained[0] = drained[0] * c_all
-                drained.append(jnp.zeros_like(m))
+                drained.append(c_all * m)
                 for c, v in enumerate(halve(drained)):
                     half[j, c, pl.ds(x * rows, rows), :] = v
             for c, v in enumerate(values):
@@ -473,11 +566,8 @@
         work(x, None)
         return carry
 
-    def rim_plane(n, carry):
-        work(n * (nx - 1), n)
-        return carry
-
-    lax.fori_loop(0, 2, rim_plane, 0)
+    work(0, 0)
+    work(nx - 1, 1)
     lax.fori_loop(1, nx // 2, planes, 0)
     if not last:
 
@@ -507,19 +597,19 @@
                 copy.wait()
 
 
-def close(k, diffusion, sums, hot, inn, st, kc, cap, mask, near, near0):
+def close(k, diffusion, sums, hot, inn, kc, cap, mask, own, near, near0):
     last = k == ITERS - 1
     nx, rows, depth = cap.shape
-    chans = st.shape[1]
+    chans = inn.shape[1]
     n_pipes = 256
-    args = [diffusion, *sums, hot, inn, st, kc, cap, mask, *near]
+    args = [diffusion, *sums, hot, inn, kc, cap, mask, *own, *near]
     if k > 0:
         args += near0
     shape = lambda *dims: jax.ShapeDtypeStruct(dims, F32)
     scratch = [
         pltpu.VMEM((2, chans, nx * rows, 128), F32),
         pltpu.VMEM((2, 4, nx * rows, 128), F32),
-        pltpu.VMEM((2, chans + 1, rows, depth), F32),
+        pltpu.VMEM((2, chans + 2, rows, depth), F32),
     ]
     if last:
         shapes = [shape(nx, rows, depth), shape(chans - 1, nx, rows, depth)]
@@ -530,7 +620,7 @@
             pltpu.SemaphoreType.DMA((nx // STEP, 2)),
         ]
     else:
-        shapes = [shape(2, nx, rows, 128), shape(*st.shape)]
+        shapes = [shape(2, nx, rows, 128), shape(2, chans, nx + 2, rows + 2 * TOP, 128)]
         shapes += [shape(chans, rows, depth)] * 2 + [shape(nx + 1, 8, n_pipes)] * 2
         out_specs = [VM] * 6
     return pl.pallas_call(
@@ -586,13 +676,11 @@
     pipe_obs,
 ):
     nx = adj_head.shape[0]
-    packs = edges(adj_head, adj_species, cond, capacity)
+    pipes = jnp.transpose(block_pipe, (0, 2, 1))
+    *packs, pa, pb, hot = first(
+        adj_head, adj_species, cond, capacity, drain_mask, pipes, pipe_obs
+    )
     near_x = beside_x(*packs)
-    block_pipe, _ = lax.optimization_barrier((block_pipe, packs))
-    st, kc, pa, pb, hot = first(
-        adj_head, adj_species, cond, capacity, drain_mask, block_pipe, pipe_obs
-    )
-    h = adj_head
     near0 = None
     sums = []
     for k in range(ITERS):
@@ -600,11 +688,17 @@
         near = near_x + near_y
         near0 = near if k == 0 else near0
         sums.append(total)
-        inn = inner(diffusion, coupling, react, st, kc, h, rate, material)
-        out = close(k, diffusion, sums, hot, inn, st, kc, capacity, drain_mask, near, near0)
+        if k == 0:
+            coef, kc, inn = first_inner(
+                diffusion, coupling, react, rate, adj_head, material, capacity, adj_species, cond
+            )
+        else:
+            inn = inner(diffusion, coupling, react, rate, h, coef, kc, st)
+        own = [*packs, pa, pb]
+        out = close(k, diffusion, sums, hot, inn, kc, capacity, drain_mask, own, near, near0)
         if k < ITERS - 1:
-            h, st, px1, px2, pa, pb = out
-            near_x = beside_x(px1, px2)
+            h, st, *packs, pa, pb = out
+            near_x = beside_x(*packs)
     return tuple(out)
 
 

time: 83 us -> 73.3 us (0.88)
  local copies, waits for them, and re-layouts: 8.73 us -> 3.13 us
  Pallas kernels: 42.6 us -> 39.4 us
  other arithmetic: 1.02 us -> 0.04 us
    unnamed x27 -> x30, local copies, waits for them, and re-layouts: 6.78 us -> 3.13 us
    pallas_call x1, Pallas kernels: 7.33 us -> 4.31 us  [first(): pl.pallas_call(functools.partial(first_kernel, nx, rows, chans), in_specs...]
    squeeze x1 -> x0, local copies, waits for them, and re-layouts: 1.06 us -> none  [pack(): return jnp.concatenate([scaled, plane(sp, 1)[:, 0], plane(cond, 0)], axis=0)]
    div x1 -> x0, other arithmetic: 0.94 us -> none  [pack(): scaled = time_step * plane(h, 0) / plane(cap, 0)]
    optimization_barrier x1 -> x0, local copies, waits for them, and re-layouts: 0.89 us -> none  [body(): block_pipe, _ = lax.optimization_barrier((block_pipe, packs))]
  transfers between devices with their start and end apart: 15 -> 15, of which waited for: 5 -> 6; matrix products, arithmetic and copies ran while one was open for 0% -> 0% of each run, Pallas kernels for 27% -> 30%
where the time goes in v1:
time: 73.3 us; the launch traced here: 72.7 us
  Pallas kernels  39.4 us (54%)
  starting transfers between devices  24.3 us (33%)
  waiting for transfers between devices  4.92 us (7%)
  local copies, waits for them, and re-layouts  3.13 us (4%)
  between operations  0.99 us (1%)
    ppermute x9, starting transfers between devices, swap(): return lax.ppermute(x, axis, pairs)  15 us
    pallas_call x3, Pallas kernels, close(): pl.pallas_call(functools.partial(close_kernel, k, last, nx, rows, chans),...  13.2 us
    pallas_call x2, Pallas kernels, inner(): pl.pallas_call(functools.partial(inner_kernel, False, nx, rows, chans), i...  11.5 us
    pallas_call x1, Pallas kernels, first_inner(): pl.pallas_call(functools.partial(inner_kernel, True, nx, rows, chans), in...  10.4 us
    ppermute x3, starting transfers between devices, beside_y(): yb = lax.ppermute(pb, 'gy', ring)  5.88 us
    pallas_call x1, Pallas kernels, first(): pl.pallas_call(functools.partial(first_kernel, nx, rows, chans), in_specs...  4.31 us
    ppermute x9, waiting for transfers between devices, swap(): return lax.ppermute(x, axis, pairs)  3.78 us
    ppermute x3, starting transfers between devices, beside_y(): lax.ppermute(four, 'gy', [(i, (i + count // 2) % count) for i in range(co...  3.4 us
  transfers between devices with their start and end apart: 15, of which 6 were waited for; matrix products, arithmetic and copies ran while one was open for 0% of the time, Pallas kernels for 30%

profile of v1, /device:TPU:6, one launch (start us, length us, event | category | flops | bytes accessed | tf_op | source)
XLA Modules:
  0.0 72.7 jit_solution(3252682165341057333)
XLA Ops:
  0.6 0.0 copy-start
  0.6 0.0 copy-start.6
  0.7 0.0 copy-start.1
  0.7 0.0 copy-start.5
  0.7 0.0 copy-start.8
  0.7 0.0 copy-start.3
  0.7 0.0 copy-start.9
  0.7 0.9 %copy-done.9 = s32[16,32,2]{1,2,0:T(2,128)S(1)} copy-done((s32[16,32,2]{1,2,0:T(2,128)S(1)}, s32[16,32,2]{1,2,0:T(2,128)}, u32[]{:S(2)}) %copy-start.9) | copy-done | bytes 4120
  1.6 0.0 copy-start.11
  1.6 1.1 %copy-done.11 = f32[7,1,32]{2,1,0:T(1,128)S(1)} copy-done((f32[7,1,32]{2,1,0:T(1,128)S(1)}, f32[7,1,32]{2,1,0:T(1,128)}, u32[]{:S(2)}) %copy-start.11) | copy-done | bytes 920
  2.7 0.0 copy-start.12
  2.7 0.0 copy-start.10
  2.7 4.3 %shard_map.131 = (f32[8,32,256]{2,1,0:T(8,128)S(1)}, f32[8,32,256]{2,1,0:T(8,128)S(1)}, f32[18,8,256]{2,1,0:T(8,128)S(1)}, f32[18,8,256]{2,1,0:T(8,128)S(1)}, bf16[2,512,256]{2,1,0:T(8,128)(2,1)}) custom-call(f32[16,32,256]{2,1,0:T(8,128)} %h.3, f32[6,16,32,256]{3,2,1,0:T(8,128)} %refs_2_.1, f32[16,32,256]{2,1,0:T(8,128)} %refs_3_.1, ...), custom_call_target="tpu_custom_call" | custom-call | flops 10000000 | bytes 8000000 | tf_op jit(solution)/shard_map/pallas_call | solution.py:205
  7.0 0.0 copy-start.2
  7.0 0.0 copy-start.4
  7.1 0.1 collective-permute-start
  7.2 1.3 %collective-permute-done.refs_13_.refs_18_.refs_19_ = f32[18,8,256]{2,1,0:T(8,128)S(1)} collective-permute-done((f32[18,8,256]{2,1,0:T(8,128)S(1)}, f32[18,8,256]{2,1,0:T(8,128)S(1)}, u32[]{:S(2)}, u32[]{:S(2)}) %collective-permute-start) | collective-permute-done | bytes 147488 | tf_op jit(solution)/shard_map/ppermute | solution.py:642
  8.5 3.8 %collective-permute-start.1 = (f32[18,8,256]{2,1,0:T(8,128)S(1)}, f32[18,8,256]{2,1,0:T(8,128)S(1)}, u32[]{:S(2)}, u32[]{:S(2)}) collective-permute-start(f32[18,8,256]{2,1,0:T(8,128)S(1)} %fusion), channel_id=1, source_target_pairs={{1,2},{2,1},{3,4},{4,3},{5,6},{6,5},{7,0},{0,7},{9,10},{10,9},{11,... | collective-permute-start | bytes 442376 | tf_op jit(solution)/shard_map/ppermute | solution.py:658
  12.3 1.6 %collective-permute-start.3 = (f32[8,32,256]{2,1,0:T(8,128)S(1)}, f32[8,32,256]{2,1,0:T(8,128)S(1)}, u32[]{:S(2)}, u32[]{:S(2)}) collective-permute-start(f32[8,32,256]{2,1,0:T(8,128)S(1)} %get-tuple-element.27.refs_7_), channel_id=1, source_target_pairs={{0,8},{8,0},{16,24},{24,16},{32,40},{40,32},{48,56},{56,48},{64,72... | collective-permute-start | bytes 786440 | tf_op jit(solution)/shard_map/ppermute | solution.py:642
  13.9 4.3 %collective-permute-start.4 = (f32[8,32,256]{2,1,0:T(8,128)S(1)}, f32[8,32,256]{2,1,0:T(8,128)S(1)}, u32[]{:S(2)}, u32[]{:S(2)}) collective-permute-start(f32[8,32,256]{2,1,0:T(8,128)S(1)} %get-tuple-element.28.refs_8_), channel_id=1, source_target_pairs={{8,16},{16,8},{24,32},{32,24},{40,48},{48,40},{56,64},{64,56},{72,... | collective-permute-start | bytes 786440 | tf_op jit(solution)/shard_map/ppermute | solution.py:642
  18.2 0.0 collective-permute-done.1.refs_14_.refs_19_.refs_20_
  18.3 0.3 collective-permute-start.2
  18.5 0.0 copy-done.12
  18.5 0.0 copy-done
  18.5 0.0 copy-done.6
  18.5 0.0 copy-done.1
  18.5 0.0 copy-done.5
  18.6 0.0 copy-done.8
  18.6 0.0 copy-done.3
  18.6 0.0 copy-done.10
  18.6 0.0 copy-start.7
  18.6 1.0 %copy-done.7 = s32[16,32,256]{2,1,0:T(8,128)S(1)} copy-done((s32[16,32,256]{2,1,0:T(8,128)S(1)}, s32[16,32,256]{2,1,0:T(8,128)}, u32[]{:S(2)}) %copy-start.7) | copy-done | bytes 524312
  19.6 10.4 %shard_map.132 = (f32[2,36,16,32,128]{4,3,2,1,0:T(8,128)S(1)}, f32[2,18,48,128]{3,2,1,0:T(8,128)S(1)}, f32[2,7,16,32,128]{4,3,2,1,0:T(8,128)S(1)}) custom-call(f32[6]{0:T(128)S(1)} %copy-done.8, f32[6]{0:T(128)S(1)} %copy-done.10, f32[4,6,6]{2,1,0:T(8,128)S(1)} %copy.14.react, f32[16,32,256]{2,1,0:T(8,128)S(1)} %copy-done.3, f32[16,32,256]{2,1,0:T(8,128)S(1)} %copy-done.5, ...), custom_call_target="tpu_custom_call" | custom-call | flops 60000000 | bytes 30000000 | tf_op jit(solution)/shard_map/pallas_call | solution.py:395
  30.0 0.0 collective-permute-done.2
  30.0 0.0 collective-permute-done.3.refs_11_.refs_16_.refs_17_
  30.0 0.0 collective-permute-done.4.refs_12_.refs_17_.refs_18_
  30.0 0.0 copy-done.2
  30.1 0.0 copy-done.4
  30.1 4.6 %shard_map.133 = (f32[2,16,32,128]{3,2,1,0:T(8,128)S(1)}, f32[2,7,18,48,128]{4,3,2,1,0:T(8,128)S(1)}, f32[7,32,256]{2,1,0:T(8,128)S(1)}, f32[7,32,256]{2,1,0:T(8...) custom-call(f32[6]{0:T(128)S(1)} %copy-done.8, f32[2,8,256]{2,1,0:T(8,128)S(1)} %add.29.refs_1_, ...), custom_call_target="tpu_custom_call" | custom-call | flops 20000000 | bytes 10000000 | tf_op jit(solution)/shard_map/pallas_call | solution.py:626
  34.7 0.8 %collective-permute-start.5 = (f32[17,8,256]{2,1,0:T(8,128)S(1)}, f32[17,8,256]{2,1,0:T(8,128)S(1)}, u32[]{:S(2)}, u32[]{:S(2)}) collective-permute-start(f32[17,8,256]{2,1,0:T(8,128)S(1)} %get-tuple-element.29.refs_10_), channel_id=1, source_target_pairs={{0,1},{1,0},{2,3},{3,2},{4,5},{5,4},{6,7},{7,6},{8,9},{9,8},{10,11... | collective-permute-start | bytes 417800 | tf_op jit(solution)/shard_map/ppermute | solution.py:642
  35.6 1.0 %collective-permute-done.5.refs_14_ = f32[17,8,256]{2,1,0:T(8,128)S(1)} collective-permute-done((f32[17,8,256]{2,1,0:T(8,128)S(1)}, f32[17,8,256]{2,1,0:T(8,128)S(1)}, u32[]{:S(2)}, u32[]{:S(2)}) %collective-permute-start.5) | collective-permute-done | bytes 139296 | tf_op jit(solution)/shard_map/ppermute | solution.py:642
  36.6 1.0 %collective-permute-start.6 = (f32[17,8,256]{2,1,0:T(8,128)S(1)}, f32[17,8,256]{2,1,0:T(8,128)S(1)}, u32[]{:S(2)}, u32[]{:S(2)}) collective-permute-start(f32[17,8,256]{2,1,0:T(8,128)S(1)} %fusion.1), channel_id=1, source_target_pairs={{1,2},{2,1},{3,4},{4,3},{5,6},{6,5},{7,0},{0,7},{9,10},{10,9},{11,... | collective-permute-start | bytes 417800 | tf_op jit(solution)/shard_map/ppermute | solution.py:658
  37.5 0.4 collective-permute-start.8
  38.0 3.7 %collective-permute-start.9 = (f32[7,32,256]{2,1,0:T(8,128)S(1)}, f32[7,32,256]{2,1,0:T(8,128)S(1)}, u32[]{:S(2)}, u32[]{:S(2)}) collective-permute-start(f32[7,32,256]{2,1,0:T(8,128)S(1)} %get-tuple-element.35.refs_9_), channel_id=1, source_target_pairs={{8,16},{16,8},{24,32},{32,24},{40,48},{48,40},{56,64},{64,56},{72,... | collective-permute-start | bytes 688136 | tf_op jit(solution)/shard_map/ppermute | solution.py:642
  41.6 0.6 collective-permute-done.6.refs_15_
  42.2 2.1 %collective-permute-start.7 = (f32[1,8,256]{2,1,0:T(8,128)S(1)}, f32[1,8,256]{2,1,0:T(8,128)S(1)}, u32[]{:S(2)}, u32[]{:S(2)}) collective-permute-start(f32[1,8,256]{2,1,0:T(8,128)S(1)} %slice_add_fusion.4), channel_id=1, source_target_pairs={{0,4},{1,5},{2,6},{3,7},{4,0},{5,1},{6,2},{7,3},{8,12},{9,13},{10,... | collective-permute-start | bytes 24584 | tf_op jit(solution)/shard_map/ppermute | solution.py:660
  44.4 5.8 %shard_map.134.refs_4_ = f32[2,7,16,32,128]{4,3,2,1,0:T(8,128)S(1)} custom-call(f32[6]{0:T(128)S(1)} %copy-done.8, f32[6]{0:T(128)S(1)} %copy-done.10, f32[4,6,6]{2,1,0:T(8,128)S(1)} %copy.14.react, f32[16,32,256]{2,1,0:T(8,128)S(1)} %copy-done.3, f32[2,16,32,128]{3,2,1,0:T(8,128)S(1)} %get-tuple-element.31.h, ...), custom_call_target="tpu_custom_call" | custom-call | flops 60000000 | bytes 30000000 | tf_op jit(solution)/shard_map/pallas_call | solution.py:379
  50.1 0.0 collective-permute-done.7
  50.2 0.0 collective-permute-done.8.refs_12_
  50.2 0.0 collective-permute-done.9.refs_13_
  50.2 4.7 %shard_map.135 = (f32[2,16,32,128]{3,2,1,0:T(8,128)S(1)}, f32[2,7,18,48,128]{4,3,2,1,0:T(8,128)S(1)}, f32[7,32,256]{2,1,0:T(8,128)S(1)}, f32[7,32,256]{2,1,0:T(8...) custom-call(f32[6]{0:T(128)S(1)} %copy-done.8, f32[2,8,256]{2,1,0:T(8,128)S(1)} %add.29.refs_1_, ...), custom_call_target="tpu_custom_call" | custom-call | flops 20000000 | bytes 10000000 | tf_op jit(solution)/shard_map/pallas_call | solution.py:626
  54.9 0.0 collective-permute-start.10
  55.0 1.3 %collective-permute-done.10.refs_15_ = f32[17,8,256]{2,1,0:T(8,128)S(1)} collective-permute-done((f32[17,8,256]{2,1,0:T(8,128)S(1)}, f32[17,8,256]{2,1,0:T(8,128)S(1)}, u32[]{:S(2)}, u32[]{:S(2)}) %collective-permute-start.10) | collective-permute-done | bytes 139296 | tf_op jit(solution)/shard_map/ppermute | solution.py:642
  56.3 1.1 %collective-permute-start.11 = (f32[17,8,256]{2,1,0:T(8,128)S(1)}, f32[17,8,256]{2,1,0:T(8,128)S(1)}, u32[]{:S(2)}, u32[]{:S(2)}) collective-permute-start(f32[17,8,256]{2,1,0:T(8,128)S(1)} %fusion.2), channel_id=1, source_target_pairs={{1,2},{2,1},{3,4},{4,3},{5,6},{6,5},{7,0},{0,7},{9,10},{10,9},{11,... | collective-permute-start | bytes 417800 | tf_op jit(solution)/shard_map/ppermute | solution.py:658
  57.4 0.0 collective-permute-start.13
  57.4 4.0 %collective-permute-start.14 = (f32[7,32,256]{2,1,0:T(8,128)S(1)}, f32[7,32,256]{2,1,0:T(8,128)S(1)}, u32[]{:S(2)}, u32[]{:S(2)}) collective-permute-start(f32[7,32,256]{2,1,0:T(8,128)S(1)} %get-tuple-element.41.refs_10_), channel_id=1, source_target_pairs={{8,16},{16,8},{24,32},{32,24},{40,48},{48,40},{56,64},{64,56},{72,... | collective-permute-start | bytes 688136 | tf_op jit(solution)/shard_map/ppermute | solution.py:642
  61.5 0.5 collective-permute-done.11.refs_16_
  62.0 1.0 %collective-permute-start.12 = (f32[1,8,256]{2,1,0:T(8,128)S(1)}, f32[1,8,256]{2,1,0:T(8,128)S(1)}, u32[]{:S(2)}, u32[]{:S(2)}) collective-permute-start(f32[1,8,256]{2,1,0:T(8,128)S(1)} %slice_add_fusion.2), channel_id=1, source_target_pairs={{0,4},{1,5},{2,6},{3,7},{4,0},{5,1},{6,2},{7,3},{8,12},{9,13},{10,... | collective-permute-start | bytes 24584 | tf_op jit(solution)/shard_map/ppermute | solution.py:660
  63.0 5.7 %shard_map.136.refs_5_ = f32[2,7,16,32,128]{4,3,2,1,0:T(8,128)S(1)} custom-call(f32[6]{0:T(128)S(1)} %copy-done.8, f32[6]{0:T(128)S(1)} %copy-done.10, f32[4,6,6]{2,1,0:T(8,128)S(1)} %copy.14.react, f32[16,32,256]{2,1,0:T(8,128)S(1)} %copy-done.3, f32[2,16,32,128]{3,2,1,0:T(8,128)S(1)} %get-tuple-element.38.h, ...), custom_call_target="tpu_custom_call" | custom-call | flops 60000000 | bytes 30000000 | tf_op jit(solution)/shard_map/pallas_call | solution.py:379
  68.8 0.0 collective-permute-done.12
  68.8 0.0 collective-permute-done.13.refs_13_
  68.8 0.1 collective-permute-done.14.refs_14_
  68.9 3.8 %shard_map.137 = (f32[16,32,256]{2,1,0:T(8,128)}, f32[6,16,32,256]{3,2,1,0:T(8,128)}) custom-call(f32[6]{0:T(128)S(1)} %copy-done.8, f32[2,8,256]{2,1,0:T(8,128)S(1)} %add.29.refs_1_, f32[1,8,256]{2,1,0:T(8,128)S(1)} %add.32.refs_2_, f32[1,8,256]{2,1,0:T(8,128)S(1)} %add.35.refs_3_, bf16[2,512,256]{2,1,0:T(8,128)(2,1)S(1)} %copy-done.4, ...), custom_call_target="tpu_custom_call" | custom-call | flops 20000000 | bytes 10000000 | tf_op jit(solution)/shard_map/pallas_call | solution.py:626
  (13 shorter events, 0.1 us)
Async XLA Ops:
  0.6 17.9 %copy-start = (f32[16,32,256]{2,1,0:T(8,128)S(1)}, f32[16,32,256]{2,1,0:T(8,128)}, u32[]{:S(2)}) copy-start(f32[16,32,256]{2,1,0:T(8,128)} %refs_7_.3) | copy-start | bytes 1572868
  0.6 17.9 %copy-start.6 = (f32[16,32,256]{2,1,0:T(8,128)S(1)}, f32[16,32,256]{2,1,0:T(8,128)}, u32[]{:S(2)}) copy-start(f32[16,32,256]{2,1,0:T(8,128)} %refs_3_.1) | copy-start | bytes 1572868
  0.7 17.9 %copy-start.1 = (f32[6,16,32,256]{3,2,1,0:T(8,128)S(1)}, f32[6,16,32,256]{3,2,1,0:T(8,128)}, u32[]{:S(2)}) copy-start(f32[6,16,32,256]{3,2,1,0:T(8,128)} %refs_2_.1) | copy-start | bytes 9437188
  0.7 17.9 %copy-start.5 = (f32[16,32,256]{2,1,0:T(8,128)S(1)}, f32[16,32,256]{2,1,0:T(8,128)}, u32[]{:S(2)}) copy-start(f32[16,32,256]{2,1,0:T(8,128)} %h.3) | copy-start | bytes 1572868
  0.7 17.9 %copy-start.8 = (f32[6]{0:T(128)S(1)}, f32[6]{0:T(128)}, u32[]{:S(2)}) copy-start(f32[6]{0:T(128)} %refs_0_.7) | copy-start | bytes 76
  0.7 17.9 %copy-start.3 = (f32[16,32,256]{2,1,0:T(8,128)S(1)}, f32[16,32,256]{2,1,0:T(8,128)}, u32[]{:S(2)}) copy-start(f32[16,32,256]{2,1,0:T(8,128)} %rate.5) | copy-start | bytes 1572868
  0.7 0.9 %copy-start.9 = (s32[16,32,2]{1,2,0:T(2,128)S(1)}, s32[16,32,2]{1,2,0:T(2,128)}, u32[]{:S(2)}) copy-start(s32[16,32,2]{1,2,0:T(2,128)} %param.22) | copy-start | bytes 12292
  1.6 1.1 %copy-start.11 = (f32[7,1,32]{2,1,0:T(1,128)S(1)}, f32[7,1,32]{2,1,0:T(1,128)}, u32[]{:S(2)}) copy-start(f32[7,1,32]{2,1,0:T(1,128)} %obs.1) | copy-start | bytes 2692
  2.7 15.8 %copy-start.12 = (f32[4,6,6]{2,0,1:T(4,128)S(1)}, f32[4,6,6]{2,0,1:T(4,128)}, u32[]{:S(2)}) copy-start(f32[4,6,6]{2,0,1:T(4,128)} %param.19) | copy-start | bytes 1732
  2.7 15.9 %copy-start.10 = (f32[6]{0:T(128)S(1)}, f32[6]{0:T(128)}, u32[]{:S(2)}) copy-start(f32[6]{0:T(128)} %coupling.5) | copy-start | bytes 76
  7.0 23.0 %copy-start.2 = (s32[16,32,256]{2,1,0:T(8,128)S(1)}, s32[16,32,256]{2,1,0:T(8,128)}, u32[]{:S(2)}) copy-start(s32[16,32,256]{2,1,0:T(8,128)} %refs_8_.1) | copy-start | bytes 1572868
  7.0 23.0 %copy-start.4 = (bf16[2,512,256]{2,1,0:T(8,128)(2,1)S(1)}, bf16[2,512,256]{2,1,0:T(8,128)(2,1)}, u32[]{:S(2)}) copy-start(bf16[2,512,256]{2,1,0:T(8,128)(2,1)} %get-tuple-element.24.refs_2_.refs_3_.refs_4_) | copy-start | bytes 1572868
  7.1 1.5 %collective-permute-start = (f32[18,8,256]{2,1,0:T(8,128)S(1)}, f32[18,8,256]{2,1,0:T(8,128)S(1)}, u32[]{:S(2)}, u32[]{:S(2)}) collective-permute-start(f32[18,8,256]{2,1,0:T(8,128)S(1)} %get-tuple-element.22.refs_9_), channel_id=1, source_target_pairs={{0,1},{1,0},{2,3},{3,2},{4,5},{5,4},{6,7},{7,6},{8,9},{9,8},{10,11... | collective-permute-start | bytes 442376 | tf_op jit(solution)/shard_map/ppermute | solution.py:642
  8.5 9.7 %collective-permute-start.1 = (f32[18,8,256]{2,1,0:T(8,128)S(1)}, f32[18,8,256]{2,1,0:T(8,128)S(1)}, u32[]{:S(2)}, u32[]{:S(2)}) collective-permute-start(f32[18,8,256]{2,1,0:T(8,128)S(1)} %fusion), channel_id=1, source_target_pairs={{1,2},{2,1},{3,4},{4,3},{5,6},{6,5},{7,0},{0,7},{9,10},{10,9},{11,... | collective-permute-start | bytes 442376 | tf_op jit(solution)/shard_map/ppermute | solution.py:658
  12.3 17.7 %collective-permute-start.3 = (f32[8,32,256]{2,1,0:T(8,128)S(1)}, f32[8,32,256]{2,1,0:T(8,128)S(1)}, u32[]{:S(2)}, u32[]{:S(2)}) collective-permute-start(f32[8,32,256]{2,1,0:T(8,128)S(1)} %get-tuple-element.27.refs_7_), channel_id=1, source_target_pairs={{0,8},{8,0},{16,24},{24,16},{32,40},{40,32},{48,56},{56,48},{64,72... | collective-permute-start | bytes 786440 | tf_op jit(solution)/shard_map/ppermute | solution.py:642
  13.9 16.2 %collective-permute-start.4 = (f32[8,32,256]{2,1,0:T(8,128)S(1)}, f32[8,32,256]{2,1,0:T(8,128)S(1)}, u32[]{:S(2)}, u32[]{:S(2)}) collective-permute-start(f32[8,32,256]{2,1,0:T(8,128)S(1)} %get-tuple-element.28.refs_8_), channel_id=1, source_target_pairs={{8,16},{16,8},{24,32},{32,24},{40,48},{48,40},{56,64},{64,56},{72,... | collective-permute-start | bytes 786440 | tf_op jit(solution)/shard_map/ppermute | solution.py:642
  18.3 11.7 %collective-permute-start.2 = (f32[2,8,256]{2,1,0:T(8,128)S(1)}, f32[2,8,256]{2,1,0:T(8,128)S(1)}, u32[]{:S(2)}, u32[]{:S(2)}) collective-permute-start(f32[2,8,256]{2,1,0:T(8,128)S(1)} %slice_add_fusion), channel_id=1, source_target_pairs={{0,4},{1,5},{2,6},{3,7},{4,0},{5,1},{6,2},{7,3},{8,12},{9,13},{10,... | collective-permute-start | bytes 49160 | tf_op jit(solution)/shard_map/ppermute | solution.py:660
  18.6 1.0 %copy-start.7 = (s32[16,32,256]{2,1,0:T(8,128)S(1)}, s32[16,32,256]{2,1,0:T(8,128)}, u32[]{:S(2)}) copy-start(s32[16,32,256]{2,1,0:T(8,128)} %refs_0_.4) | copy-start | bytes 1572868
  34.7 1.8 %collective-permute-start.5 = (f32[17,8,256]{2,1,0:T(8,128)S(1)}, f32[17,8,256]{2,1,0:T(8,128)S(1)}, u32[]{:S(2)}, u32[]{:S(2)}) collective-permute-start(f32[17,8,256]{2,1,0:T(8,128)S(1)} %get-tuple-element.29.refs_10_), channel_id=1, source_target_pairs={{0,1},{1,0},{2,3},{3,2},{4,5},{5,4},{6,7},{7,6},{8,9},{9,8},{10,11... | collective-permute-start | bytes 417800 | tf_op jit(solution)/shard_map/ppermute | solution.py:642
  36.6 5.7 %collective-permute-start.6 = (f32[17,8,256]{2,1,0:T(8,128)S(1)}, f32[17,8,256]{2,1,0:T(8,128)S(1)}, u32[]{:S(2)}, u32[]{:S(2)}) collective-permute-start(f32[17,8,256]{2,1,0:T(8,128)S(1)} %fusion.1), channel_id=1, source_target_pairs={{1,2},{2,1},{3,4},{4,3},{5,6},{6,5},{7,0},{0,7},{9,10},{10,9},{11,... | collective-permute-start | bytes 417800 | tf_op jit(solution)/shard_map/ppermute | solution.py:658
  37.5 12.6 %collective-permute-start.8 = (f32[7,32,256]{2,1,0:T(8,128)S(1)}, f32[7,32,256]{2,1,0:T(8,128)S(1)}, u32[]{:S(2)}, u32[]{:S(2)}) collective-permute-start(f32[7,32,256]{2,1,0:T(8,128)S(1)} %get-tuple-element.34.refs_8_), channel_id=1, source_target_pairs={{0,8},{8,0},{16,24},{24,16},{32,40},{40,32},{48,56},{56,48},{64,72... | collective-permute-start | bytes 688136 | tf_op jit(solution)/shard_map/ppermute | solution.py:642
  38.0 12.2 %collective-permute-start.9 = (f32[7,32,256]{2,1,0:T(8,128)S(1)}, f32[7,32,256]{2,1,0:T(8,128)S(1)}, u32[]{:S(2)}, u32[]{:S(2)}) collective-permute-start(f32[7,32,256]{2,1,0:T(8,128)S(1)} %get-tuple-element.35.refs_9_), channel_id=1, source_target_pairs={{8,16},{16,8},{24,32},{32,24},{40,48},{48,40},{56,64},{64,56},{72,... | collective-permute-start | bytes 688136 | tf_op jit(solution)/shard_map/ppermute | solution.py:642
  42.2 7.9 %collective-permute-start.7 = (f32[1,8,256]{2,1,0:T(8,128)S(1)}, f32[1,8,256]{2,1,0:T(8,128)S(1)}, u32[]{:S(2)}, u32[]{:S(2)}) collective-permute-start(f32[1,8,256]{2,1,0:T(8,128)S(1)} %slice_add_fusion.4), channel_id=1, source_target_pairs={{0,4},{1,5},{2,6},{3,7},{4,0},{5,1},{6,2},{7,3},{8,12},{9,13},{10,... | collective-permute-start | bytes 24584 | tf_op jit(solution)/shard_map/ppermute | solution.py:660
  54.9 1.4 %collective-permute-start.10 = (f32[17,8,256]{2,1,0:T(8,128)S(1)}, f32[17,8,256]{2,1,0:T(8,128)S(1)}, u32[]{:S(2)}, u32[]{:S(2)}) collective-permute-start(f32[17,8,256]{2,1,0:T(8,128)S(1)} %get-tuple-element.36.refs_11_), channel_id=1, source_target_pairs={{0,1},{1,0},{2,3},{3,2},{4,5},{5,4},{6,7},{7,6},{8,9},{9,8},{10,11... | collective-permute-start | bytes 417800 | tf_op jit(solution)/shard_map/ppermute | solution.py:642
  56.3 5.7 %collective-permute-start.11 = (f32[17,8,256]{2,1,0:T(8,128)S(1)}, f32[17,8,256]{2,1,0:T(8,128)S(1)}, u32[]{:S(2)}, u32[]{:S(2)}) collective-permute-start(f32[17,8,256]{2,1,0:T(8,128)S(1)} %fusion.2), channel_id=1, source_target_pairs={{1,2},{2,1},{3,4},{4,3},{5,6},{6,5},{7,0},{0,7},{9,10},{10,9},{11,... | collective-permute-start | bytes 417800 | tf_op jit(solution)/shard_map/ppermute | solution.py:658
  57.4 11.4 %collective-permute-start.13 = (f32[7,32,256]{2,1,0:T(8,128)S(1)}, f32[7,32,256]{2,1,0:T(8,128)S(1)}, u32[]{:S(2)}, u32[]{:S(2)}) collective-permute-start(f32[7,32,256]{2,1,0:T(8,128)S(1)} %get-tuple-element.40.refs_9_), channel_id=1, source_target_pairs={{0,8},{8,0},{16,24},{24,16},{32,40},{40,32},{48,56},{56,48},{64,72... | collective-permute-start | bytes 688136 | tf_op jit(solution)/shard_map/ppermute | solution.py:642
  57.4 11.5 %collective-permute-start.14 = (f32[7,32,256]{2,1,0:T(8,128)S(1)}, f32[7,32,256]{2,1,0:T(8,128)S(1)}, u32[]{:S(2)}, u32[]{:S(2)}) collective-permute-start(f32[7,32,256]{2,1,0:T(8,128)S(1)} %get-tuple-element.41.refs_10_), channel_id=1, source_target_pairs={{8,16},{16,8},{24,32},{32,24},{40,48},{48,40},{56,64},{64,56},{72,... | collective-permute-start | bytes 688136 | tf_op jit(solution)/shard_map/ppermute | solution.py:642
  62.0 6.8 %collective-permute-start.12 = (f32[1,8,256]{2,1,0:T(8,128)S(1)}, f32[1,8,256]{2,1,0:T(8,128)S(1)}, u32[]{:S(2)}, u32[]{:S(2)}) collective-permute-start(f32[1,8,256]{2,1,0:T(8,128)S(1)} %slice_add_fusion.2), channel_id=1, source_target_pairs={{0,4},{1,5},{2,6},{3,7},{4,0},{5,1},{6,2},{7,3},{8,12},{9,13},{10,... | collective-permute-start | bytes 24584 | tf_op jit(solution)/shard_map/ppermute | solution.py:660

commit v2 on v1

--- a/solution.py
+++ b/solution.py
@@ -230,13 +230,17 @@
     )(h, sp, cond, cap, mask, bp, obs)
 
 
-def inner_kernel(fresh, nx, rows, chans, diffusion, coupling, react, rate, h, *refs):
+def inner_kernel(fresh, nx, rows, chans, diffusion, coupling, *refs):
     if fresh:
-        mat, cap, sp, cond, coef, kc, out, st, vh, vcap, sem = refs
+        react, rate, h, mat, cap, sp, cond, coef, kc, out, st, vh, vcap, sem = refs
     else:
-        coef, kc, st, out = refs
+        rate, h, coef, kc, st, out = refs
     nsp = chans - 1
     both = range(2)
+    gains = diffusion[...].reshape(1, nsp)
+    heads = coupling[...].reshape(1, nsp)
+    diffusion = [jnp.broadcast_to(gains[:, c : c + 1], (RB, 128)) for c in range(nsp)]
+    coupling = [jnp.broadcast_to(heads[:, c : c + 1], (RB, 128)) for c in range(nsp)]
     lane = lax.broadcasted_iota(jnp.int32, (RB, 128), 1)
     first_lane, last_lane = lane == 0, lane == 127
 
@@ -288,14 +292,24 @@
         arrive(0)
         scale(0)
         scale(1)
-
-    def plane(x, carry):
+        scale(2)
+
+    def planes(i, carry):
+        x = 2 * i
         if fresh:
 
-            @pl.when((x % STEP == STEP - 2) & (x < nx - 2))
+            @pl.when((x % STEP == 0) & (x < nx - STEP))
             def _():
                 arrive(x // STEP + 1)
 
+        plane(x)
+        plane(x + 1)
+        if fresh:
+            scale(jnp.minimum(x + 3, nx - 1))
+            scale(jnp.minimum(x + 4, nx - 1))
+        return carry
+
+    def plane(x):
         for r in range(0, rows, RB):
             at = TOP + r
             body = slice(r, r + RB)
@@ -366,11 +380,8 @@
                         acc[j] = acc[j] + w * mids[t][j]
                 for j in both:
                     out[j, s + 1, x, body, :] = acc[j]
-        if fresh:
-            scale(jnp.minimum(x + 2, nx - 1))
-        return carry
-
-    lax.fori_loop(0, nx, plane, 0)
+
+    lax.fori_loop(0, nx // 2, planes, 0)
 
 
 def inner(diffusion, coupling, react, rate, h, coef, kc, st):
@@ -378,12 +389,12 @@
     chans = st.shape[1]
     return pl.pallas_call(
         functools.partial(inner_kernel, False, nx, rows, chans),
-        in_specs=[SM] * 3 + [VM] * 5,
+        in_specs=[VM] * 2 + [VM] * 5,
         out_specs=VM,
         out_shape=jax.ShapeDtypeStruct((2, chans, nx, rows, 128), F32),
         compiler_params=pltpu.CompilerParams(vmem_limit_bytes=2 * 2**20),
         cost_estimate=pl.CostEstimate(flops=6 * 10**7, bytes_accessed=3 * 10**7, transcendentals=0),
-    )(diffusion, coupling, react, rate, h, coef, kc, st)
+    )(diffusion, coupling, rate, h, coef, kc, st)
 
 
 def first_inner(diffusion, coupling, react, rate, h, mat, cap, sp, cond):
@@ -394,7 +405,7 @@
     padded = (nx + 2, rows + 2 * TOP, 128)
     return pl.pallas_call(
         functools.partial(inner_kernel, True, nx, rows, chans),
-        in_specs=[SM] * 3 + [VM, HB, VM, HB, HB, HB],
+        in_specs=[VM, VM, SM, VM, HB, VM, HB, HB, HB],
         out_specs=[VM] * 3,
         out_shape=[
             shape(2, nsp * nsp, nx, rows, 128),
@@ -464,8 +475,10 @@
     row = lax.broadcasted_iota(jnp.int32, (8, 128), 0)
     top, bottom = row == 0, row == 7
     gains = jnp.zeros((8, 128), F32)
+    share = time_step * diffusion[...].reshape(1, nsp)
+    shares = [share[:, c : c + 1] for c in range(nsp)]
     for c in range(nsp):
-        gains = jnp.where(row == c + 1, time_step * diffusion[c], gains)
+        gains = jnp.where(row == c + 1, shares[c], gains)
     rim = jnp.zeros((TOP, 128), F32)
     if not last:
         for c in range(chans):
@@ -522,7 +535,7 @@
                     if c == 0:
                         v = v + pull(c_all, xh[rim_at, chans + 1, :, part], xh[rim_at, chans, :, part], far)
                     else:
-                        v = v + time_step * diffusion[c - 1] * far
+                        v = v + shares[c - 1] * far
                 values.append(v)
             if not last:
                 drained = [v * m for v in values]
@@ -625,7 +638,7 @@
         out_specs = [VM] * 6
     return pl.pallas_call(
         functools.partial(close_kernel, k, last, nx, rows, chans),
-        in_specs=[SM] + [VM] * (len(args) - 1),
+        in_specs=[VM] * len(args),
         out_specs=out_specs,
         out_shape=shapes,
         scratch_shapes=scratch,

time: 73.3 us -> 71.2 us (0.971)
  Pallas kernels: 39.4 us -> 35.9 us
  waiting for transfers between devices: 4.92 us -> 6.28 us
    pallas_call x2, Pallas kernels: 11.5 us -> 9.81 us  [inner(): pl.pallas_call(functools.partial(inner_kernel, False, nx, rows, chans), i...]
    pallas_call x3, Pallas kernels: 13.2 us -> 11.6 us  [close(): pl.pallas_call(functools.partial(close_kernel, k, last, nx, rows, chans),...]
    ppermute x9, waiting for transfers between devices: 3.78 us -> 5.21 us  [swap(): return lax.ppermute(x, axis, pairs)]
  transfers between devices with their start and end apart: 15 -> 15, of which waited for: 6 -> 6; matrix products, arithmetic and copies ran while one was open for 0% -> 0% of each run, Pallas kernels for 30% -> 28%
where the time goes in v2:
time: 71.2 us; the launch traced here: 70.9 us
  Pallas kernels  35.9 us (50%)
  starting transfers between devices  24.6 us (35%)
  waiting for transfers between devices  6.28 us (9%)
  local copies, waits for them, and re-layouts  3.14 us (4%)
  between operations  0.98 us (1%)
    ppermute x9, starting transfers between devices, swap(): return lax.ppermute(x, axis, pairs)  14.5 us
    pallas_call x3, Pallas kernels, close(): pl.pallas_call(functools.partial(close_kernel, k, last, nx, rows, chans),...  11.6 us
    pallas_call x1, Pallas kernels, first_inner(): pl.pallas_call(functools.partial(inner_kernel, True, nx, rows, chans), in...  10.1 us
    pallas_call x2, Pallas kernels, inner(): pl.pallas_call(functools.partial(inner_kernel, False, nx, rows, chans), i...  9.81 us
    ppermute x3, starting transfers between devices, beside_y(): yb = lax.ppermute(pb, 'gy', ring)  6.47 us
    ppermute x9, waiting for transfers between devices, swap(): return lax.ppermute(x, axis, pairs)  5.21 us
    pallas_call x1, Pallas kernels, first(): pl.pallas_call(functools.partial(first_kernel, nx, rows, chans), in_specs...  4.31 us
    ppermute x3, starting transfers between devices, beside_y(): lax.ppermute(four, 'gy', [(i, (i + count // 2) % count) for i in range(co...  3.67 us
  transfers between devices with their start and end apart: 15, of which 6 were waited for; matrix products, arithmetic and copies ran while one was open for 0% of the time, Pallas kernels for 28%

profile of v2, /device:TPU:6, one launch (start us, length us, event | category | flops | bytes accessed | tf_op | source)
XLA Modules:
  0.0 70.9 jit_solution(16448529694029839644)
XLA Ops:
  0.6 0.0 copy-start
  0.6 0.0 copy-start.6
  0.7 0.0 copy-start.1
  0.7 0.0 copy-start.5
  0.7 0.0 copy-start.8
  0.7 0.0 copy-start.3
  0.7 0.0 copy-start.9
  0.7 0.9 %copy-done.9 = s32[16,32,2]{1,2,0:T(2,128)S(1)} copy-done((s32[16,32,2]{1,2,0:T(2,128)S(1)}, s32[16,32,2]{1,2,0:T(2,128)}, u32[]{:S(2)}) %copy-start.9) | copy-done | bytes 4120
  1.6 0.0 copy-start.11
  1.6 1.1 %copy-done.11 = f32[7,1,32]{2,1,0:T(1,128)S(1)} copy-done((f32[7,1,32]{2,1,0:T(1,128)S(1)}, f32[7,1,32]{2,1,0:T(1,128)}, u32[]{:S(2)}) %copy-start.11) | copy-done | bytes 920
  2.7 0.0 copy-start.12
  2.7 0.0 copy-start.10
  2.7 4.3 %shard_map.131 = (f32[8,32,256]{2,1,0:T(8,128)S(1)}, f32[8,32,256]{2,1,0:T(8,128)S(1)}, f32[18,8,256]{2,1,0:T(8,128)S(1)}, f32[18,8,256]{2,1,0:T(8,128)S(1)}, bf16[2,512,256]{2,1,0:T(8,128)(2,1)}) custom-call(f32[16,32,256]{2,1,0:T(8,128)} %refs_2_.1, f32[6,16,32,256]{3,2,1,0:T(8,128)} %refs_5_.2, f32[16,32,256]{2,1,0:T(8,128)} %refs_6_.3, ...), custom_call_target="tpu_custom_call" | custom-call | flops 10000000 | bytes 8000000 | tf_op jit(solution)/shard_map/pallas_call | solution.py:205
  7.0 0.0 copy-start.2
  7.0 0.0 copy-start.4
  7.1 0.1 collective-permute-start
  7.2 1.3 %collective-permute-done.refs_13_.refs_18_.refs_19_ = f32[18,8,256]{2,1,0:T(8,128)S(1)} collective-permute-done((f32[18,8,256]{2,1,0:T(8,128)S(1)}, f32[18,8,256]{2,1,0:T(8,128)S(1)}, u32[]{:S(2)}, u32[]{:S(2)}) %collective-permute-start) | collective-permute-done | bytes 147488 | tf_op jit(solution)/shard_map/ppermute | solution.py:655
  8.5 3.8 %collective-permute-start.1 = (f32[18,8,256]{2,1,0:T(8,128)S(1)}, f32[18,8,256]{2,1,0:T(8,128)S(1)}, u32[]{:S(2)}, u32[]{:S(2)}) collective-permute-start(f32[18,8,256]{2,1,0:T(8,128)S(1)} %fusion), channel_id=1, source_target_pairs={{1,2},{2,1},{3,4},{4,3},{5,6},{6,5},{7,0},{0,7},{9,10},{10,9},{11,... | collective-permute-start | bytes 442376 | tf_op jit(solution)/shard_map/ppermute | solution.py:671
  12.3 1.6 %collective-permute-start.3 = (f32[8,32,256]{2,1,0:T(8,128)S(1)}, f32[8,32,256]{2,1,0:T(8,128)S(1)}, u32[]{:S(2)}, u32[]{:S(2)}) collective-permute-start(f32[8,32,256]{2,1,0:T(8,128)S(1)} %get-tuple-element.27.refs_7_), channel_id=1, source_target_pairs={{0,8},{8,0},{16,24},{24,16},{32,40},{40,32},{48,56},{56,48},{64,72... | collective-permute-start | bytes 786440 | tf_op jit(solution)/shard_map/ppermute | solution.py:655
  13.9 4.3 %collective-permute-start.4 = (f32[8,32,256]{2,1,0:T(8,128)S(1)}, f32[8,32,256]{2,1,0:T(8,128)S(1)}, u32[]{:S(2)}, u32[]{:S(2)}) collective-permute-start(f32[8,32,256]{2,1,0:T(8,128)S(1)} %get-tuple-element.28.refs_8_), channel_id=1, source_target_pairs={{8,16},{16,8},{24,32},{32,24},{40,48},{48,40},{56,64},{64,56},{72,... | collective-permute-start | bytes 786440 | tf_op jit(solution)/shard_map/ppermute | solution.py:655
  18.2 0.0 collective-permute-done.1.refs_14_.refs_19_.refs_20_
  18.3 0.3 collective-permute-start.2
  18.5 0.0 copy-done.12
  18.5 0.0 copy-done
  18.5 0.0 copy-done.6
  18.5 0.0 copy-done.1
  18.5 0.0 copy-done.5
  18.6 0.0 copy-done.8
  18.6 0.0 copy-done.3
  18.6 0.0 copy-done.10
  18.6 0.0 copy-start.7
  18.6 1.0 %copy-done.7 = s32[16,32,256]{2,1,0:T(8,128)S(1)} copy-done((s32[16,32,256]{2,1,0:T(8,128)S(1)}, s32[16,32,256]{2,1,0:T(8,128)}, u32[]{:S(2)}) %copy-start.7) | copy-done | bytes 524312
  19.6 10.1 %shard_map.132 = (f32[2,36,16,32,128]{4,3,2,1,0:T(8,128)S(1)}, f32[2,18,48,128]{3,2,1,0:T(8,128)S(1)}, f32[2,7,16,32,128]{4,3,2,1,0:T(8,128)S(1)}) custom-call(f32[6]{0:T(128)S(1)} %copy-done.8, f32[6]{0:T(128)S(1)} %copy-done.10, f32[4,6,6]{2,1,0:T(8,128)S(1)} %copy.14.refs_0_, f32[16,32,256]{2,1,0:T(8,128)S(1)} %copy-done.3, f32[16,32,256]{2,1,0:T(8,128)S(1)} %copy-done.5, ...), custom_call_target="tpu_custom_call" | custom-call | flops 60000000 | bytes 30000000 | tf_op jit(solution)/shard_map/pallas_call | solution.py:406
  29.8 0.0 collective-permute-done.2
  29.8 0.0 collective-permute-done.3.refs_11_.refs_16_.refs_17_
  29.8 0.0 collective-permute-done.4.refs_12_.refs_17_.refs_18_
  29.8 0.0 copy-done.2
  29.8 0.0 copy-done.4
  29.8 4.1 %shard_map.133 = (f32[2,16,32,128]{3,2,1,0:T(8,128)S(1)}, f32[2,7,18,48,128]{4,3,2,1,0:T(8,128)S(1)}, f32[7,32,256]{2,1,0:T(8,128)S(1)}, f32[7,32,256]{2,1,0:T(8...) custom-call(f32[6]{0:T(128)S(1)} %copy-done.8, f32[2,8,256]{2,1,0:T(8,128)S(1)} %add.29.refs_1_, ...), custom_call_target="tpu_custom_call" | custom-call | flops 20000000 | bytes 10000000 | tf_op jit(solution)/shard_map/pallas_call | solution.py:639
  33.9 0.8 %collective-permute-start.5 = (f32[17,8,256]{2,1,0:T(8,128)S(1)}, f32[17,8,256]{2,1,0:T(8,128)S(1)}, u32[]{:S(2)}, u32[]{:S(2)}) collective-permute-start(f32[17,8,256]{2,1,0:T(8,128)S(1)} %get-tuple-element.29.refs_10_), channel_id=1, source_target_pairs={{0,1},{1,0},{2,3},{3,2},{4,5},{5,4},{6,7},{7,6},{8,9},{9,8},{10,11... | collective-permute-start | bytes 417800 | tf_op jit(solution)/shard_map/ppermute | solution.py:655
  34.8 1.0 %collective-permute-done.5.refs_14_ = f32[17,8,256]{2,1,0:T(8,128)S(1)} collective-permute-done((f32[17,8,256]{2,1,0:T(8,128)S(1)}, f32[17,8,256]{2,1,0:T(8,128)S(1)}, u32[]{:S(2)}, u32[]{:S(2)}) %collective-permute-start.5) | collective-permute-done | bytes 139296 | tf_op jit(solution)/shard_map/ppermute | solution.py:655
  35.8 1.0 %collective-permute-start.6 = (f32[17,8,256]{2,1,0:T(8,128)S(1)}, f32[17,8,256]{2,1,0:T(8,128)S(1)}, u32[]{:S(2)}, u32[]{:S(2)}) collective-permute-start(f32[17,8,256]{2,1,0:T(8,128)S(1)} %fusion.1), channel_id=1, source_target_pairs={{1,2},{2,1},{3,4},{4,3},{5,6},{6,5},{7,0},{0,7},{9,10},{10,9},{11,... | collective-permute-start | bytes 417800 | tf_op jit(solution)/shard_map/ppermute | solution.py:671
  36.7 0.4 collective-permute-start.8
  37.2 3.7 %collective-permute-start.9 = (f32[7,32,256]{2,1,0:T(8,128)S(1)}, f32[7,32,256]{2,1,0:T(8,128)S(1)}, u32[]{:S(2)}, u32[]{:S(2)}) collective-permute-start(f32[7,32,256]{2,1,0:T(8,128)S(1)} %get-tuple-element.35.refs_9_), channel_id=1, source_target_pairs={{8,16},{16,8},{24,32},{32,24},{40,48},{48,40},{56,64},{64,56},{72,... | collective-permute-start | bytes 688136 | tf_op jit(solution)/shard_map/ppermute | solution.py:655
  40.9 0.6 collective-permute-done.6.refs_15_
  41.5 2.1 %collective-permute-start.7 = (f32[1,8,256]{2,1,0:T(8,128)S(1)}, f32[1,8,256]{2,1,0:T(8,128)S(1)}, u32[]{:S(2)}, u32[]{:S(2)}) collective-permute-start(f32[1,8,256]{2,1,0:T(8,128)S(1)} %slice_add_fusion.4), channel_id=1, source_target_pairs={{0,4},{1,5},{2,6},{3,7},{4,0},{5,1},{6,2},{7,3},{8,12},{9,13},{10,... | collective-permute-start | bytes 24584 | tf_op jit(solution)/shard_map/ppermute | solution.py:673
  43.6 5.2 %shard_map.134.refs_4_ = f32[2,7,16,32,128]{4,3,2,1,0:T(8,128)S(1)} custom-call(f32[6]{0:T(128)S(1)} %copy-done.8, f32[6]{0:T(128)S(1)} %copy-done.10, f32[16,32,256]{2,1,0:T(8,128)S(1)} %copy-done.3, f32[2,16,32,128]{3,2,1,0:T(8,128)S(1)} %get-tuple-element.31.refs_1_, f32[2,36,16,32,128]{4,3,2,1,0:T(8,128)S(1)} %get-tuple-element.32.refs_2_, ...), custom_call_target="tpu_custom_call" | custom-call | flops 60000000 | bytes 30000000 | tf_op jit(solution)/shard_map/pallas_call | solution.py:390
  48.8 0.0 collective-permute-done.7
  48.8 0.0 collective-permute-done.8.refs_12_
  48.8 0.0 collective-permute-done.9.refs_13_
  48.8 4.2 %shard_map.135 = (f32[2,16,32,128]{3,2,1,0:T(8,128)S(1)}, f32[2,7,18,48,128]{4,3,2,1,0:T(8,128)S(1)}, f32[7,32,256]{2,1,0:T(8,128)S(1)}, f32[7,32,256]{2,1,0:T(8...) custom-call(f32[6]{0:T(128)S(1)} %copy-done.8, f32[2,8,256]{2,1,0:T(8,128)S(1)} %add.29.refs_1_, ...), custom_call_target="tpu_custom_call" | custom-call | flops 20000000 | bytes 10000000 | tf_op jit(solution)/shard_map/pallas_call | solution.py:639
  53.0 0.0 collective-permute-start.10
  53.1 1.3 %collective-permute-done.10.refs_15_ = f32[17,8,256]{2,1,0:T(8,128)S(1)} collective-permute-done((f32[17,8,256]{2,1,0:T(8,128)S(1)}, f32[17,8,256]{2,1,0:T(8,128)S(1)}, u32[]{:S(2)}, u32[]{:S(2)}) %collective-permute-start.10) | collective-permute-done | bytes 139296 | tf_op jit(solution)/shard_map/ppermute | solution.py:655
  54.4 1.7 %collective-permute-start.11 = (f32[17,8,256]{2,1,0:T(8,128)S(1)}, f32[17,8,256]{2,1,0:T(8,128)S(1)}, u32[]{:S(2)}, u32[]{:S(2)}) collective-permute-start(f32[17,8,256]{2,1,0:T(8,128)S(1)} %fusion.2), channel_id=1, source_target_pairs={{1,2},{2,1},{3,4},{4,3},{5,6},{6,5},{7,0},{0,7},{9,10},{10,9},{11,... | collective-permute-start | bytes 417800 | tf_op jit(solution)/shard_map/ppermute | solution.py:671
  56.1 0.0 collective-permute-start.13
  56.1 3.5 %collective-permute-start.14 = (f32[7,32,256]{2,1,0:T(8,128)S(1)}, f32[7,32,256]{2,1,0:T(8,128)S(1)}, u32[]{:S(2)}, u32[]{:S(2)}) collective-permute-start(f32[7,32,256]{2,1,0:T(8,128)S(1)} %get-tuple-element.41.refs_10_), channel_id=1, source_target_pairs={{8,16},{16,8},{24,32},{32,24},{40,48},{48,40},{56,64},{64,56},{72,... | collective-permute-start | bytes 688136 | tf_op jit(solution)/shard_map/ppermute | solution.py:655
  59.6 0.5 collective-permute-done.11.refs_16_
  60.1 1.3 %collective-permute-start.12 = (f32[1,8,256]{2,1,0:T(8,128)S(1)}, f32[1,8,256]{2,1,0:T(8,128)S(1)}, u32[]{:S(2)}, u32[]{:S(2)}) collective-permute-start(f32[1,8,256]{2,1,0:T(8,128)S(1)} %slice_add_fusion.2), channel_id=1, source_target_pairs={{0,4},{1,5},{2,6},{3,7},{4,0},{5,1},{6,2},{7,3},{8,12},{9,13},{10,... | collective-permute-start | bytes 24584 | tf_op jit(solution)/shard_map/ppermute | solution.py:673
  61.4 4.6 %shard_map.136.refs_5_ = f32[2,7,16,32,128]{4,3,2,1,0:T(8,128)S(1)} custom-call(f32[6]{0:T(128)S(1)} %copy-done.8, f32[6]{0:T(128)S(1)} %copy-done.10, f32[16,32,256]{2,1,0:T(8,128)S(1)} %copy-done.3, f32[2,16,32,128]{3,2,1,0:T(8,128)S(1)} %get-tuple-element.38.refs_1_, f32[2,36,16,32,128]{4,3,2,1,0:T(8,128)S(1)} %get-tuple-element.32.refs_2_, ...), custom_call_target="tpu_custom_call" | custom-call | flops 60000000 | bytes 30000000 | tf_op jit(solution)/shard_map/pallas_call | solution.py:390
  66.0 0.0 collective-permute-done.12
  66.1 0.0 collective-permute-done.13.refs_13_
  66.1 1.5 %collective-permute-done.14.refs_14_ = f32[7,32,256]{2,1,0:T(8,128)S(1)} collective-permute-done((f32[7,32,256]{2,1,0:T(8,128)S(1)}, f32[7,32,256]{2,1,0:T(8,128)S(1)}, u32[]{:S(2)}, u32[]{:S(2)}) %collective-permute-start.14) | collective-permute-done | bytes 229408 | tf_op jit(solution)/shard_map/ppermute | solution.py:655
  67.6 3.3 %shard_map.137 = (f32[16,32,256]{2,1,0:T(8,128)}, f32[6,16,32,256]{3,2,1,0:T(8,128)}) custom-call(f32[6]{0:T(128)S(1)} %copy-done.8, f32[2,8,256]{2,1,0:T(8,128)S(1)} %add.29.refs_1_, f32[1,8,256]{2,1,0:T(8,128)S(1)} %add.32.refs_2_, f32[1,8,256]{2,1,0:T(8,128)S(1)} %add.35.refs_3_, bf16[2,512,256]{2,1,0:T(8,128)(2,1)S(1)} %copy-done.4, ...), custom_call_target="tpu_custom_call" | custom-call | flops 20000000 | bytes 10000000 | tf_op jit(solution)/shard_map/pallas_call | solution.py:639
  (13 shorter events, 0.1 us)
Async XLA Ops:
  0.6 17.9 %copy-start = (f32[16,32,256]{2,1,0:T(8,128)S(1)}, f32[16,32,256]{2,1,0:T(8,128)}, u32[]{:S(2)}) copy-start(f32[16,32,256]{2,1,0:T(8,128)} %refs_7_.3) | copy-start | bytes 1572868
  0.6 17.9 %copy-start.6 = (f32[16,32,256]{2,1,0:T(8,128)S(1)}, f32[16,32,256]{2,1,0:T(8,128)}, u32[]{:S(2)}) copy-start(f32[16,32,256]{2,1,0:T(8,128)} %refs_6_.3) | copy-start | bytes 1572868
  0.7 17.9 %copy-start.1 = (f32[6,16,32,256]{3,2,1,0:T(8,128)S(1)}, f32[6,16,32,256]{3,2,1,0:T(8,128)}, u32[]{:S(2)}) copy-start(f32[6,16,32,256]{3,2,1,0:T(8,128)} %refs_5_.2) | copy-start | bytes 9437188
  0.7 17.9 %copy-start.5 = (f32[16,32,256]{2,1,0:T(8,128)S(1)}, f32[16,32,256]{2,1,0:T(8,128)}, u32[]{:S(2)}) copy-start(f32[16,32,256]{2,1,0:T(8,128)} %refs_2_.1) | copy-start | bytes 1572868
  0.7 17.9 %copy-start.8 = (f32[6]{0:T(128)S(1)}, f32[6]{0:T(128)}, u32[]{:S(2)}) copy-start(f32[6]{0:T(128)} %refs_0_.10) | copy-start | bytes 76
  0.7 17.9 %copy-start.3 = (f32[16,32,256]{2,1,0:T(8,128)S(1)}, f32[16,32,256]{2,1,0:T(8,128)}, u32[]{:S(2)}) copy-start(f32[16,32,256]{2,1,0:T(8,128)} %refs_0_.9) | copy-start | bytes 1572868
  0.7 0.9 %copy-start.9 = (s32[16,32,2]{1,2,0:T(2,128)S(1)}, s32[16,32,2]{1,2,0:T(2,128)}, u32[]{:S(2)}) copy-start(s32[16,32,2]{1,2,0:T(2,128)} %param.22) | copy-start | bytes 12292
  1.6 1.1 %copy-start.11 = (f32[7,1,32]{2,1,0:T(1,128)S(1)}, f32[7,1,32]{2,1,0:T(1,128)}, u32[]{:S(2)}) copy-start(f32[7,1,32]{2,1,0:T(1,128)} %obs.1) | copy-start | bytes 2692
  2.7 15.8 %copy-start.12 = (f32[4,6,6]{2,0,1:T(4,128)S(1)}, f32[4,6,6]{2,0,1:T(4,128)}, u32[]{:S(2)}) copy-start(f32[4,6,6]{2,0,1:T(4,128)} %param.19) | copy-start | bytes 1732
  2.7 15.9 %copy-start.10 = (f32[6]{0:T(128)S(1)}, f32[6]{0:T(128)}, u32[]{:S(2)}) copy-start(f32[6]{0:T(128)} %coupling.5) | copy-start | bytes 76
  7.0 22.8 %copy-start.2 = (s32[16,32,256]{2,1,0:T(8,128)S(1)}, s32[16,32,256]{2,1,0:T(8,128)}, u32[]{:S(2)}) copy-start(s32[16,32,256]{2,1,0:T(8,128)} %refs_8_.1) | copy-start | bytes 1572868
  7.0 22.8 %copy-start.4 = (bf16[2,512,256]{2,1,0:T(8,128)(2,1)S(1)}, bf16[2,512,256]{2,1,0:T(8,128)(2,1)}, u32[]{:S(2)}) copy-start(bf16[2,512,256]{2,1,0:T(8,128)(2,1)} %get-tuple-element.24.refs_2_.refs_3_.refs_4_) | copy-start | bytes 1572868
  7.1 1.5 %collective-permute-start = (f32[18,8,256]{2,1,0:T(8,128)S(1)}, f32[18,8,256]{2,1,0:T(8,128)S(1)}, u32[]{:S(2)}, u32[]{:S(2)}) collective-permute-start(f32[18,8,256]{2,1,0:T(8,128)S(1)} %get-tuple-element.22.refs_9_), channel_id=1, source_target_pairs={{0,1},{1,0},{2,3},{3,2},{4,5},{5,4},{6,7},{7,6},{8,9},{9,8},{10,11... | collective-permute-start | bytes 442376 | tf_op jit(solution)/shard_map/ppermute | solution.py:655
  8.5 9.7 %collective-permute-start.1 = (f32[18,8,256]{2,1,0:T(8,128)S(1)}, f32[18,8,256]{2,1,0:T(8,128)S(1)}, u32[]{:S(2)}, u32[]{:S(2)}) collective-permute-start(f32[18,8,256]{2,1,0:T(8,128)S(1)} %fusion), channel_id=1, source_target_pairs={{1,2},{2,1},{3,4},{4,3},{5,6},{6,5},{7,0},{0,7},{9,10},{10,9},{11,... | collective-permute-start | bytes 442376 | tf_op jit(solution)/shard_map/ppermute | solution.py:671
  12.3 17.5 %collective-permute-start.3 = (f32[8,32,256]{2,1,0:T(8,128)S(1)}, f32[8,32,256]{2,1,0:T(8,128)S(1)}, u32[]{:S(2)}, u32[]{:S(2)}) collective-permute-start(f32[8,32,256]{2,1,0:T(8,128)S(1)} %get-tuple-element.27.refs_7_), channel_id=1, source_target_pairs={{0,8},{8,0},{16,24},{24,16},{32,40},{40,32},{48,56},{56,48},{64,72... | collective-permute-start | bytes 786440 | tf_op jit(solution)/shard_map/ppermute | solution.py:655
  13.9 15.9 %collective-permute-start.4 = (f32[8,32,256]{2,1,0:T(8,128)S(1)}, f32[8,32,256]{2,1,0:T(8,128)S(1)}, u32[]{:S(2)}, u32[]{:S(2)}) collective-permute-start(f32[8,32,256]{2,1,0:T(8,128)S(1)} %get-tuple-element.28.refs_8_), channel_id=1, source_target_pairs={{8,16},{16,8},{24,32},{32,24},{40,48},{48,40},{56,64},{64,56},{72,... | collective-permute-start | bytes 786440 | tf_op jit(solution)/shard_map/ppermute | solution.py:655
  18.3 11.5 %collective-permute-start.2 = (f32[2,8,256]{2,1,0:T(8,128)S(1)}, f32[2,8,256]{2,1,0:T(8,128)S(1)}, u32[]{:S(2)}, u32[]{:S(2)}) collective-permute-start(f32[2,8,256]{2,1,0:T(8,128)S(1)} %slice_add_fusion), channel_id=1, source_target_pairs={{0,4},{1,5},{2,6},{3,7},{4,0},{5,1},{6,2},{7,3},{8,12},{9,13},{10,... | collective-permute-start | bytes 49160 | tf_op jit(solution)/shard_map/ppermute | solution.py:673
  18.6 1.0 %copy-start.7 = (s32[16,32,256]{2,1,0:T(8,128)S(1)}, s32[16,32,256]{2,1,0:T(8,128)}, u32[]{:S(2)}) copy-start(s32[16,32,256]{2,1,0:T(8,128)} %refs_3_.1) | copy-start | bytes 1572868
  33.9 1.8 %collective-permute-start.5 = (f32[17,8,256]{2,1,0:T(8,128)S(1)}, f32[17,8,256]{2,1,0:T(8,128)S(1)}, u32[]{:S(2)}, u32[]{:S(2)}) collective-permute-start(f32[17,8,256]{2,1,0:T(8,128)S(1)} %get-tuple-element.29.refs_10_), channel_id=1, source_target_pairs={{0,1},{1,0},{2,3},{3,2},{4,5},{5,4},{6,7},{7,6},{8,9},{9,8},{10,11... | collective-permute-start | bytes 417800 | tf_op jit(solution)/shard_map/ppermute | solution.py:655
  35.8 5.7 %collective-permute-start.6 = (f32[17,8,256]{2,1,0:T(8,128)S(1)}, f32[17,8,256]{2,1,0:T(8,128)S(1)}, u32[]{:S(2)}, u32[]{:S(2)}) collective-permute-start(f32[17,8,256]{2,1,0:T(8,128)S(1)} %fusion.1), channel_id=1, source_target_pairs={{1,2},{2,1},{3,4},{4,3},{5,6},{6,5},{7,0},{0,7},{9,10},{10,9},{11,... | collective-permute-start | bytes 417800 | tf_op jit(solution)/shard_map/ppermute | solution.py:671
  36.7 12.0 %collective-permute-start.8 = (f32[7,32,256]{2,1,0:T(8,128)S(1)}, f32[7,32,256]{2,1,0:T(8,128)S(1)}, u32[]{:S(2)}, u32[]{:S(2)}) collective-permute-start(f32[7,32,256]{2,1,0:T(8,128)S(1)} %get-tuple-element.34.refs_8_), channel_id=1, source_target_pairs={{0,8},{8,0},{16,24},{24,16},{32,40},{40,32},{48,56},{56,48},{64,72... | collective-permute-start | bytes 688136 | tf_op jit(solution)/shard_map/ppermute | solution.py:655
  37.2 11.6 %collective-permute-start.9 = (f32[7,32,256]{2,1,0:T(8,128)S(1)}, f32[7,32,256]{2,1,0:T(8,128)S(1)}, u32[]{:S(2)}, u32[]{:S(2)}) collective-permute-start(f32[7,32,256]{2,1,0:T(8,128)S(1)} %get-tuple-element.35.refs_9_), channel_id=1, source_target_pairs={{8,16},{16,8},{24,32},{32,24},{40,48},{48,40},{56,64},{64,56},{72,... | collective-permute-start | bytes 688136 | tf_op jit(solution)/shard_map/ppermute | solution.py:655
  41.5 7.3 %collective-permute-start.7 = (f32[1,8,256]{2,1,0:T(8,128)S(1)}, f32[1,8,256]{2,1,0:T(8,128)S(1)}, u32[]{:S(2)}, u32[]{:S(2)}) collective-permute-start(f32[1,8,256]{2,1,0:T(8,128)S(1)} %slice_add_fusion.4), channel_id=1, source_target_pairs={{0,4},{1,5},{2,6},{3,7},{4,0},{5,1},{6,2},{7,3},{8,12},{9,13},{10,... | collective-permute-start | bytes 24584 | tf_op jit(solution)/shard_map/ppermute | solution.py:673
  53.0 1.4 %collective-permute-start.10 = (f32[17,8,256]{2,1,0:T(8,128)S(1)}, f32[17,8,256]{2,1,0:T(8,128)S(1)}, u32[]{:S(2)}, u32[]{:S(2)}) collective-permute-start(f32[17,8,256]{2,1,0:T(8,128)S(1)} %get-tuple-element.36.refs_11_), channel_id=1, source_target_pairs={{0,1},{1,0},{2,3},{3,2},{4,5},{5,4},{6,7},{7,6},{8,9},{9,8},{10,11... | collective-permute-start | bytes 417800 | tf_op jit(solution)/shard_map/ppermute | solution.py:655
  54.4 5.7 %collective-permute-start.11 = (f32[17,8,256]{2,1,0:T(8,128)S(1)}, f32[17,8,256]{2,1,0:T(8,128)S(1)}, u32[]{:S(2)}, u32[]{:S(2)}) collective-permute-start(f32[17,8,256]{2,1,0:T(8,128)S(1)} %fusion.2), channel_id=1, source_target_pairs={{1,2},{2,1},{3,4},{4,3},{5,6},{6,5},{7,0},{0,7},{9,10},{10,9},{11,... | collective-permute-start | bytes 417800 | tf_op jit(solution)/shard_map/ppermute | solution.py:671
  56.1 10.0 %collective-permute-start.13 = (f32[7,32,256]{2,1,0:T(8,128)S(1)}, f32[7,32,256]{2,1,0:T(8,128)S(1)}, u32[]{:S(2)}, u32[]{:S(2)}) collective-permute-start(f32[7,32,256]{2,1,0:T(8,128)S(1)} %get-tuple-element.40.refs_9_), channel_id=1, source_target_pairs={{0,8},{8,0},{16,24},{24,16},{32,40},{40,32},{48,56},{56,48},{64,72... | collective-permute-start | bytes 688136 | tf_op jit(solution)/shard_map/ppermute | solution.py:655
  56.1 11.5 %collective-permute-start.14 = (f32[7,32,256]{2,1,0:T(8,128)S(1)}, f32[7,32,256]{2,1,0:T(8,128)S(1)}, u32[]{:S(2)}, u32[]{:S(2)}) collective-permute-start(f32[7,32,256]{2,1,0:T(8,128)S(1)} %get-tuple-element.41.refs_10_), channel_id=1, source_target_pairs={{8,16},{16,8},{24,32},{32,24},{40,48},{48,40},{56,64},{64,56},{72,... | collective-permute-start | bytes 688136 | tf_op jit(solution)/shard_map/ppermute | solution.py:655
  60.1 5.9 %collective-permute-start.12 = (f32[1,8,256]{2,1,0:T(8,128)S(1)}, f32[1,8,256]{2,1,0:T(8,128)S(1)}, u32[]{:S(2)}, u32[]{:S(2)}) collective-permute-start(f32[1,8,256]{2,1,0:T(8,128)S(1)} %slice_add_fusion.2), channel_id=1, source_target_pairs={{0,4},{1,5},{2,6},{3,7},{4,0},{5,1},{6,2},{7,3},{8,12},{9,13},{10,... | collective-permute-start | bytes 24584 | tf_op jit(solution)/shard_map/ppermute | solution.py:673

commit v3 on v2

--- a/solution.py
+++ b/solution.py
@@ -19,6 +19,7 @@
 SM = pl.BlockSpec(memory_space=pltpu.SMEM)
 TOP = 8
 STEP = 4
+INNER_STEP = 8
 RB = 16
 
 
@@ -252,7 +253,7 @@
         return up, down
 
     def chunk(g):
-        at, into = pl.ds(g * STEP, STEP), pl.ds(g * STEP + 1, STEP)
+        at, into = pl.ds(g * INNER_STEP, INNER_STEP), pl.ds(g * INNER_STEP + 1, INNER_STEP)
         inside = pl.ds(TOP, rows)
         pairs = []
         for j, part in enumerate((pl.ds(0, 128), pl.ds(128, 128))):
@@ -272,7 +273,7 @@
             st[j, 0, x + 1, TOP : TOP + rows, :] = scaled
 
     if fresh:
-        for g in range(nx // STEP):
+        for g in range(nx // INNER_STEP):
             for copy in chunk(g):
                 copy.start()
         for c in range(chans):
@@ -298,9 +299,9 @@
         x = 2 * i
         if fresh:
 
-            @pl.when((x % STEP == 0) & (x < nx - STEP))
+            @pl.when((x % INNER_STEP == 0) & (x < nx - INNER_STEP))
             def _():
-                arrive(x // STEP + 1)
+                arrive(x // INNER_STEP + 1)
 
         plane(x)
         plane(x + 1)
@@ -416,7 +417,7 @@
             pltpu.VMEM((2, chans, *padded), F32),
             pltpu.VMEM((nx, rows, depth), F32),
             pltpu.VMEM((nx, rows, depth), F32),
-            pltpu.SemaphoreType.DMA((nx // STEP, 6)),
+            pltpu.SemaphoreType.DMA((nx // INNER_STEP, 6)),
         ],
         compiler_params=pltpu.CompilerParams(vmem_limit_bytes=12 * 2**20),
         cost_estimate=pl.CostEstimate(flops=6 * 10**7, bytes_accessed=3 * 10**7, transcendentals=0),

time: 71.2 us -> 69.9 us (0.982)
  Pallas kernels: 35.9 us -> 34.5 us
    pallas_call x1, Pallas kernels: 10.1 us -> 8.72 us  [first_inner(): pl.pallas_call(functools.partial(inner_kernel, True, nx, rows, chans), in...]
  transfers between devices with their start and end apart: 15 -> 15, of which waited for: 6 -> 6; matrix products, arithmetic and copies ran while one was open for 0% -> 0% of each run, Pallas kernels for 28% -> 27%
where the time goes in v3:
time: 69.9 us; the launch traced here: 69.5 us
  Pallas kernels  34.5 us (49%)
  starting transfers between devices  24.6 us (35%)
  waiting for transfers between devices  6.28 us (9%)
  local copies, waits for them, and re-layouts  3.14 us (4%)
  between operations  0.98 us (1%)
    ppermute x9, starting transfers between devices, swap(): return lax.ppermute(x, axis, pairs)  14.4 us
    pallas_call x3, Pallas kernels, close(): pl.pallas_call(functools.partial(close_kernel, k, last, nx, rows, chans),...  11.6 us
    pallas_call x2, Pallas kernels, inner(): pl.pallas_call(functools.partial(inner_kernel, False, nx, rows, chans), i...  9.81 us
    pallas_call x1, Pallas kernels, first_inner(): pl.pallas_call(functools.partial(inner_kernel, True, nx, rows, chans), in...  8.72 us
    ppermute x3, starting transfers between devices, beside_y(): yb = lax.ppermute(pb, 'gy', ring)  6.48 us
    ppermute x9, waiting for transfers between devices, swap(): return lax.ppermute(x, axis, pairs)  5.21 us
    pallas_call x1, Pallas kernels, first(): pl.pallas_call(functools.partial(first_kernel, nx, rows, chans), in_specs...  4.31 us
    ppermute x3, starting transfers between devices, beside_y(): lax.ppermute(four, 'gy', [(i, (i + count // 2) % count) for i in range(co...  3.67 us
  transfers between devices with their start and end apart: 15, of which 6 were waited for; matrix products, arithmetic and copies ran while one was open for 0% of the time, Pallas kernels for 27%

profile of v3, /device:TPU:6, one launch (start us, length us, event | category | flops | bytes accessed | tf_op | source)
XLA Modules:
  0.0 69.5 jit_solution(7288017554677839683)
XLA Ops:
  0.6 0.0 copy-start
  0.6 0.0 copy-start.6
  0.7 0.0 copy-start.1
  0.7 0.0 copy-start.5
  0.7 0.0 copy-start.8
  0.7 0.0 copy-start.3
  0.7 0.0 copy-start.9
  0.7 0.9 %copy-done.9 = s32[16,32,2]{1,2,0:T(2,128)S(1)} copy-done((s32[16,32,2]{1,2,0:T(2,128)S(1)}, s32[16,32,2]{1,2,0:T(2,128)}, u32[]{:S(2)}) %copy-start.9) | copy-done | bytes 4120
  1.6 0.0 copy-start.11
  1.6 1.1 %copy-done.11 = f32[7,1,32]{2,1,0:T(1,128)S(1)} copy-done((f32[7,1,32]{2,1,0:T(1,128)S(1)}, f32[7,1,32]{2,1,0:T(1,128)}, u32[]{:S(2)}) %copy-start.11) | copy-done | bytes 920
  2.7 0.0 copy-start.12
  2.7 0.0 copy-start.10
  2.7 4.3 %shard_map.131 = (f32[8,32,256]{2,1,0:T(8,128)S(1)}, f32[8,32,256]{2,1,0:T(8,128)S(1)}, f32[18,8,256]{2,1,0:T(8,128)S(1)}, f32[18,8,256]{2,1,0:T(8,128)S(1)}, bf16[2,512,256]{2,1,0:T(8,128)(2,1)}) custom-call(f32[16,32,256]{2,1,0:T(8,128)} %refs_2_.1, f32[6,16,32,256]{3,2,1,0:T(8,128)} %refs_5_.2, f32[16,32,256]{2,1,0:T(8,128)} %refs_6_.3, ...), custom_call_target="tpu_custom_call" | custom-call | flops 10000000 | bytes 8000000 | tf_op jit(solution)/shard_map/pallas_call | solution.py:206
  7.0 0.0 copy-start.2
  7.0 0.0 copy-start.4
  7.1 0.1 collective-permute-start
  7.2 1.3 %collective-permute-done.refs_13_.refs_18_.refs_19_ = f32[18,8,256]{2,1,0:T(8,128)S(1)} collective-permute-done((f32[18,8,256]{2,1,0:T(8,128)S(1)}, f32[18,8,256]{2,1,0:T(8,128)S(1)}, u32[]{:S(2)}, u32[]{:S(2)}) %collective-permute-start) | collective-permute-done | bytes 147488 | tf_op jit(solution)/shard_map/ppermute | solution.py:656
  8.5 3.8 %collective-permute-start.1 = (f32[18,8,256]{2,1,0:T(8,128)S(1)}, f32[18,8,256]{2,1,0:T(8,128)S(1)}, u32[]{:S(2)}, u32[]{:S(2)}) collective-permute-start(f32[18,8,256]{2,1,0:T(8,128)S(1)} %fusion), channel_id=1, source_target_pairs={{1,2},{2,1},{3,4},{4,3},{5,6},{6,5},{7,0},{0,7},{9,10},{10,9},{11,... | collective-permute-start | bytes 442376 | tf_op jit(solution)/shard_map/ppermute | solution.py:672
  12.3 1.6 %collective-permute-start.3 = (f32[8,32,256]{2,1,0:T(8,128)S(1)}, f32[8,32,256]{2,1,0:T(8,128)S(1)}, u32[]{:S(2)}, u32[]{:S(2)}) collective-permute-start(f32[8,32,256]{2,1,0:T(8,128)S(1)} %get-tuple-element.27.refs_7_), channel_id=1, source_target_pairs={{0,8},{8,0},{16,24},{24,16},{32,40},{40,32},{48,56},{56,48},{64,72... | collective-permute-start | bytes 786440 | tf_op jit(solution)/shard_map/ppermute | solution.py:656
  13.9 4.3 %collective-permute-start.4 = (f32[8,32,256]{2,1,0:T(8,128)S(1)}, f32[8,32,256]{2,1,0:T(8,128)S(1)}, u32[]{:S(2)}, u32[]{:S(2)}) collective-permute-start(f32[8,32,256]{2,1,0:T(8,128)S(1)} %get-tuple-element.28.refs_8_), channel_id=1, source_target_pairs={{8,16},{16,8},{24,32},{32,24},{40,48},{48,40},{56,64},{64,56},{72,... | collective-permute-start | bytes 786440 | tf_op jit(solution)/shard_map/ppermute | solution.py:656
  18.2 0.0 collective-permute-done.1.refs_14_.refs_19_.refs_20_
  18.3 0.3 collective-permute-start.2
  18.5 0.0 copy-done.12
  18.5 0.0 copy-done
  18.5 0.0 copy-done.6
  18.5 0.0 copy-done.1
  18.5 0.0 copy-done.5
  18.6 0.0 copy-done.8
  18.6 0.0 copy-done.3
  18.6 0.0 copy-done.10
  18.6 0.0 copy-start.7
  18.6 1.0 %copy-done.7 = s32[16,32,256]{2,1,0:T(8,128)S(1)} copy-done((s32[16,32,256]{2,1,0:T(8,128)S(1)}, s32[16,32,256]{2,1,0:T(8,128)}, u32[]{:S(2)}) %copy-start.7) | copy-done | bytes 524312
  19.6 8.7 %shard_map.132 = (f32[2,36,16,32,128]{4,3,2,1,0:T(8,128)S(1)}, f32[2,18,48,128]{3,2,1,0:T(8,128)S(1)}, f32[2,7,16,32,128]{4,3,2,1,0:T(8,128)S(1)}) custom-call(f32[6]{0:T(128)S(1)} %copy-done.8, f32[6]{0:T(128)S(1)} %copy-done.10, f32[4,6,6]{2,1,0:T(8,128)S(1)} %copy.14.refs_0_, f32[16,32,256]{2,1,0:T(8,128)S(1)} %copy-done.3, f32[16,32,256]{2,1,0:T(8,128)S(1)} %copy-done.5, ...), custom_call_target="tpu_custom_call" | custom-call | flops 60000000 | bytes 30000000 | tf_op jit(solution)/shard_map/pallas_call | solution.py:407
  28.4 0.0 collective-permute-done.2
  28.4 0.0 collective-permute-done.3.refs_11_.refs_16_.refs_17_
  28.4 0.0 collective-permute-done.4.refs_12_.refs_17_.refs_18_
  28.4 0.0 copy-done.2
  28.4 0.0 copy-done.4
  28.4 4.1 %shard_map.133 = (f32[2,16,32,128]{3,2,1,0:T(8,128)S(1)}, f32[2,7,18,48,128]{4,3,2,1,0:T(8,128)S(1)}, f32[7,32,256]{2,1,0:T(8,128)S(1)}, f32[7,32,256]{2,1,0:T(8...) custom-call(f32[6]{0:T(128)S(1)} %copy-done.8, f32[2,8,256]{2,1,0:T(8,128)S(1)} %add.29.refs_1_, ...), custom_call_target="tpu_custom_call" | custom-call | flops 20000000 | bytes 10000000 | tf_op jit(solution)/shard_map/pallas_call | solution.py:640
  32.5 0.8 %collective-permute-start.5 = (f32[17,8,256]{2,1,0:T(8,128)S(1)}, f32[17,8,256]{2,1,0:T(8,128)S(1)}, u32[]{:S(2)}, u32[]{:S(2)}) collective-permute-start(f32[17,8,256]{2,1,0:T(8,128)S(1)} %get-tuple-element.29.refs_10_), channel_id=1, source_target_pairs={{0,1},{1,0},{2,3},{3,2},{4,5},{5,4},{6,7},{7,6},{8,9},{9,8},{10,11... | collective-permute-start | bytes 417800 | tf_op jit(solution)/shard_map/ppermute | solution.py:656
  33.4 1.0 %collective-permute-done.5.refs_14_ = f32[17,8,256]{2,1,0:T(8,128)S(1)} collective-permute-done((f32[17,8,256]{2,1,0:T(8,128)S(1)}, f32[17,8,256]{2,1,0:T(8,128)S(1)}, u32[]{:S(2)}, u32[]{:S(2)}) %collective-permute-start.5) | collective-permute-done | bytes 139296 | tf_op jit(solution)/shard_map/ppermute | solution.py:656
  34.4 1.0 %collective-permute-start.6 = (f32[17,8,256]{2,1,0:T(8,128)S(1)}, f32[17,8,256]{2,1,0:T(8,128)S(1)}, u32[]{:S(2)}, u32[]{:S(2)}) collective-permute-start(f32[17,8,256]{2,1,0:T(8,128)S(1)} %fusion.1), channel_id=1, source_target_pairs={{1,2},{2,1},{3,4},{4,3},{5,6},{6,5},{7,0},{0,7},{9,10},{10,9},{11,... | collective-permute-start | bytes 417800 | tf_op jit(solution)/shard_map/ppermute | solution.py:672
  35.4 0.4 collective-permute-start.8
  35.8 3.7 %collective-permute-start.9 = (f32[7,32,256]{2,1,0:T(8,128)S(1)}, f32[7,32,256]{2,1,0:T(8,128)S(1)}, u32[]{:S(2)}, u32[]{:S(2)}) collective-permute-start(f32[7,32,256]{2,1,0:T(8,128)S(1)} %get-tuple-element.35.refs_9_), channel_id=1, source_target_pairs={{8,16},{16,8},{24,32},{32,24},{40,48},{48,40},{56,64},{64,56},{72,... | collective-permute-start | bytes 688136 | tf_op jit(solution)/shard_map/ppermute | solution.py:656
  39.5 0.6 collective-permute-done.6.refs_15_
  40.1 2.1 %collective-permute-start.7 = (f32[1,8,256]{2,1,0:T(8,128)S(1)}, f32[1,8,256]{2,1,0:T(8,128)S(1)}, u32[]{:S(2)}, u32[]{:S(2)}) collective-permute-start(f32[1,8,256]{2,1,0:T(8,128)S(1)} %slice_add_fusion.4), channel_id=1, source_target_pairs={{0,4},{1,5},{2,6},{3,7},{4,0},{5,1},{6,2},{7,3},{8,12},{9,13},{10,... | collective-permute-start | bytes 24584 | tf_op jit(solution)/shard_map/ppermute | solution.py:674
  42.2 5.2 %shard_map.134.refs_4_ = f32[2,7,16,32,128]{4,3,2,1,0:T(8,128)S(1)} custom-call(f32[6]{0:T(128)S(1)} %copy-done.8, f32[6]{0:T(128)S(1)} %copy-done.10, f32[16,32,256]{2,1,0:T(8,128)S(1)} %copy-done.3, f32[2,16,32,128]{3,2,1,0:T(8,128)S(1)} %get-tuple-element.31.refs_1_, f32[2,36,16,32,128]{4,3,2,1,0:T(8,128)S(1)} %get-tuple-element.32.refs_2_, ...), custom_call_target="tpu_custom_call" | custom-call | flops 60000000 | bytes 30000000 | tf_op jit(solution)/shard_map/pallas_call | solution.py:391
  47.4 0.0 collective-permute-done.7
  47.4 0.0 collective-permute-done.8.refs_12_
  47.4 0.0 collective-permute-done.9.refs_13_
  47.4 4.2 %shard_map.135 = (f32[2,16,32,128]{3,2,1,0:T(8,128)S(1)}, f32[2,7,18,48,128]{4,3,2,1,0:T(8,128)S(1)}, f32[7,32,256]{2,1,0:T(8,128)S(1)}, f32[7,32,256]{2,1,0:T(8...) custom-call(f32[6]{0:T(128)S(1)} %copy-done.8, f32[2,8,256]{2,1,0:T(8,128)S(1)} %add.29.refs_1_, ...), custom_call_target="tpu_custom_call" | custom-call | flops 20000000 | bytes 10000000 | tf_op jit(solution)/shard_map/pallas_call | solution.py:640
  51.6 0.0 collective-permute-start.10
  51.7 1.3 %collective-permute-done.10.refs_15_ = f32[17,8,256]{2,1,0:T(8,128)S(1)} collective-permute-done((f32[17,8,256]{2,1,0:T(8,128)S(1)}, f32[17,8,256]{2,1,0:T(8,128)S(1)}, u32[]{:S(2)}, u32[]{:S(2)}) %collective-permute-start.10) | collective-permute-done | bytes 139296 | tf_op jit(solution)/shard_map/ppermute | solution.py:656
  53.0 1.7 %collective-permute-start.11 = (f32[17,8,256]{2,1,0:T(8,128)S(1)}, f32[17,8,256]{2,1,0:T(8,128)S(1)}, u32[]{:S(2)}, u32[]{:S(2)}) collective-permute-start(f32[17,8,256]{2,1,0:T(8,128)S(1)} %fusion.2), channel_id=1, source_target_pairs={{1,2},{2,1},{3,4},{4,3},{5,6},{6,5},{7,0},{0,7},{9,10},{10,9},{11,... | collective-permute-start | bytes 417800 | tf_op jit(solution)/shard_map/ppermute | solution.py:672
  54.7 0.0 collective-permute-start.13
  54.7 3.5 %collective-permute-start.14 = (f32[7,32,256]{2,1,0:T(8,128)S(1)}, f32[7,32,256]{2,1,0:T(8,128)S(1)}, u32[]{:S(2)}, u32[]{:S(2)}) collective-permute-start(f32[7,32,256]{2,1,0:T(8,128)S(1)} %get-tuple-element.41.refs_10_), channel_id=1, source_target_pairs={{8,16},{16,8},{24,32},{32,24},{40,48},{48,40},{56,64},{64,56},{72,... | collective-permute-start | bytes 688136 | tf_op jit(solution)/shard_map/ppermute | solution.py:656
  58.2 0.5 collective-permute-done.11.refs_16_
  58.7 1.3 %collective-permute-start.12 = (f32[1,8,256]{2,1,0:T(8,128)S(1)}, f32[1,8,256]{2,1,0:T(8,128)S(1)}, u32[]{:S(2)}, u32[]{:S(2)}) collective-permute-start(f32[1,8,256]{2,1,0:T(8,128)S(1)} %slice_add_fusion.2), channel_id=1, source_target_pairs={{0,4},{1,5},{2,6},{3,7},{4,0},{5,1},{6,2},{7,3},{8,12},{9,13},{10,... | collective-permute-start | bytes 24584 | tf_op jit(solution)/shard_map/ppermute | solution.py:674
  60.0 4.6 %shard_map.136.refs_5_ = f32[2,7,16,32,128]{4,3,2,1,0:T(8,128)S(1)} custom-call(f32[6]{0:T(128)S(1)} %copy-done.8, f32[6]{0:T(128)S(1)} %copy-done.10, f32[16,32,256]{2,1,0:T(8,128)S(1)} %copy-done.3, f32[2,16,32,128]{3,2,1,0:T(8,128)S(1)} %get-tuple-element.38.refs_1_, f32[2,36,16,32,128]{4,3,2,1,0:T(8,128)S(1)} %get-tuple-element.32.refs_2_, ...), custom_call_target="tpu_custom_call" | custom-call | flops 60000000 | bytes 30000000 | tf_op jit(solution)/shard_map/pallas_call | solution.py:391
  64.6 0.0 collective-permute-done.12
  64.7 0.0 collective-permute-done.13.refs_13_
  64.7 1.5 %collective-permute-done.14.refs_14_ = f32[7,32,256]{2,1,0:T(8,128)S(1)} collective-permute-done((f32[7,32,256]{2,1,0:T(8,128)S(1)}, f32[7,32,256]{2,1,0:T(8,128)S(1)}, u32[]{:S(2)}, u32[]{:S(2)}) %collective-permute-start.14) | collective-permute-done | bytes 229408 | tf_op jit(solution)/shard_map/ppermute | solution.py:656
  66.2 3.3 %shard_map.137 = (f32[16,32,256]{2,1,0:T(8,128)}, f32[6,16,32,256]{3,2,1,0:T(8,128)}) custom-call(f32[6]{0:T(128)S(1)} %copy-done.8, f32[2,8,256]{2,1,0:T(8,128)S(1)} %add.29.refs_1_, f32[1,8,256]{2,1,0:T(8,128)S(1)} %add.32.refs_2_, f32[1,8,256]{2,1,0:T(8,128)S(1)} %add.35.refs_3_, bf16[2,512,256]{2,1,0:T(8,128)(2,1)S(1)} %copy-done.4, ...), custom_call_target="tpu_custom_call" | custom-call | flops 20000000 | bytes 10000000 | tf_op jit(solution)/shard_map/pallas_call | solution.py:640
  (13 shorter events, 0.1 us)
Async XLA Ops:
  0.6 17.9 %copy-start = (f32[16,32,256]{2,1,0:T(8,128)S(1)}, f32[16,32,256]{2,1,0:T(8,128)}, u32[]{:S(2)}) copy-start(f32[16,32,256]{2,1,0:T(8,128)} %refs_7_.3) | copy-start | bytes 1572868
  0.6 17.9 %copy-start.6 = (f32[16,32,256]{2,1,0:T(8,128)S(1)}, f32[16,32,256]{2,1,0:T(8,128)}, u32[]{:S(2)}) copy-start(f32[16,32,256]{2,1,0:T(8,128)} %refs_6_.3) | copy-start | bytes 1572868
  0.7 17.9 %copy-start.1 = (f32[6,16,32,256]{3,2,1,0:T(8,128)S(1)}, f32[6,16,32,256]{3,2,1,0:T(8,128)}, u32[]{:S(2)}) copy-start(f32[6,16,32,256]{3,2,1,0:T(8,128)} %refs_5_.2) | copy-start | bytes 9437188
  0.7 17.9 %copy-start.5 = (f32[16,32,256]{2,1,0:T(8,128)S(1)}, f32[16,32,256]{2,1,0:T(8,128)}, u32[]{:S(2)}) copy-start(f32[16,32,256]{2,1,0:T(8,128)} %refs_2_.1) | copy-start | bytes 1572868
  0.7 17.9 %copy-start.8 = (f32[6]{0:T(128)S(1)}, f32[6]{0:T(128)}, u32[]{:S(2)}) copy-start(f32[6]{0:T(128)} %refs_0_.10) | copy-start | bytes 76
  0.7 17.9 %copy-start.3 = (f32[16,32,256]{2,1,0:T(8,128)S(1)}, f32[16,32,256]{2,1,0:T(8,128)}, u32[]{:S(2)}) copy-start(f32[16,32,256]{2,1,0:T(8,128)} %refs_0_.9) | copy-start | bytes 1572868
  0.7 0.9 %copy-start.9 = (s32[16,32,2]{1,2,0:T(2,128)S(1)}, s32[16,32,2]{1,2,0:T(2,128)}, u32[]{:S(2)}) copy-start(s32[16,32,2]{1,2,0:T(2,128)} %param.22) | copy-start | bytes 12292
  1.6 1.1 %copy-start.11 = (f32[7,1,32]{2,1,0:T(1,128)S(1)}, f32[7,1,32]{2,1,0:T(1,128)}, u32[]{:S(2)}) copy-start(f32[7,1,32]{2,1,0:T(1,128)} %obs.1) | copy-start | bytes 2692
  2.7 15.8 %copy-start.12 = (f32[4,6,6]{2,0,1:T(4,128)S(1)}, f32[4,6,6]{2,0,1:T(4,128)}, u32[]{:S(2)}) copy-start(f32[4,6,6]{2,0,1:T(4,128)} %param.19) | copy-start | bytes 1732
  2.7 15.9 %copy-start.10 = (f32[6]{0:T(128)S(1)}, f32[6]{0:T(128)}, u32[]{:S(2)}) copy-start(f32[6]{0:T(128)} %coupling.5) | copy-start | bytes 76
  7.0 21.4 %copy-start.2 = (s32[16,32,256]{2,1,0:T(8,128)S(1)}, s32[16,32,256]{2,1,0:T(8,128)}, u32[]{:S(2)}) copy-start(s32[16,32,256]{2,1,0:T(8,128)} %refs_8_.1) | copy-start | bytes 1572868
  7.0 21.4 %copy-start.4 = (bf16[2,512,256]{2,1,0:T(8,128)(2,1)S(1)}, bf16[2,512,256]{2,1,0:T(8,128)(2,1)}, u32[]{:S(2)}) copy-start(bf16[2,512,256]{2,1,0:T(8,128)(2,1)} %get-tuple-element.24.refs_2_.refs_3_.refs_4_) | copy-start | bytes 1572868
  7.1 1.5 %collective-permute-start = (f32[18,8,256]{2,1,0:T(8,128)S(1)}, f32[18,8,256]{2,1,0:T(8,128)S(1)}, u32[]{:S(2)}, u32[]{:S(2)}) collective-permute-start(f32[18,8,256]{2,1,0:T(8,128)S(1)} %get-tuple-element.22.refs_9_), channel_id=1, source_target_pairs={{0,1},{1,0},{2,3},{3,2},{4,5},{5,4},{6,7},{7,6},{8,9},{9,8},{10,11... | collective-permute-start | bytes 442376 | tf_op jit(solution)/shard_map/ppermute | solution.py:656
  8.5 9.7 %collective-permute-start.1 = (f32[18,8,256]{2,1,0:T(8,128)S(1)}, f32[18,8,256]{2,1,0:T(8,128)S(1)}, u32[]{:S(2)}, u32[]{:S(2)}) collective-permute-start(f32[18,8,256]{2,1,0:T(8,128)S(1)} %fusion), channel_id=1, source_target_pairs={{1,2},{2,1},{3,4},{4,3},{5,6},{6,5},{7,0},{0,7},{9,10},{10,9},{11,... | collective-permute-start | bytes 442376 | tf_op jit(solution)/shard_map/ppermute | solution.py:672
  12.3 16.1 %collective-permute-start.3 = (f32[8,32,256]{2,1,0:T(8,128)S(1)}, f32[8,32,256]{2,1,0:T(8,128)S(1)}, u32[]{:S(2)}, u32[]{:S(2)}) collective-permute-start(f32[8,32,256]{2,1,0:T(8,128)S(1)} %get-tuple-element.27.refs_7_), channel_id=1, source_target_pairs={{0,8},{8,0},{16,24},{24,16},{32,40},{40,32},{48,56},{56,48},{64,72... | collective-permute-start | bytes 786440 | tf_op jit(solution)/shard_map/ppermute | solution.py:656
  13.9 14.5 %collective-permute-start.4 = (f32[8,32,256]{2,1,0:T(8,128)S(1)}, f32[8,32,256]{2,1,0:T(8,128)S(1)}, u32[]{:S(2)}, u32[]{:S(2)}) collective-permute-start(f32[8,32,256]{2,1,0:T(8,128)S(1)} %get-tuple-element.28.refs_8_), channel_id=1, source_target_pairs={{8,16},{16,8},{24,32},{32,24},{40,48},{48,40},{56,64},{64,56},{72,... | collective-permute-start | bytes 786440 | tf_op jit(solution)/shard_map/ppermute | solution.py:656
  18.3 10.1 %collective-permute-start.2 = (f32[2,8,256]{2,1,0:T(8,128)S(1)}, f32[2,8,256]{2,1,0:T(8,128)S(1)}, u32[]{:S(2)}, u32[]{:S(2)}) collective-permute-start(f32[2,8,256]{2,1,0:T(8,128)S(1)} %slice_add_fusion), channel_id=1, source_target_pairs={{0,4},{1,5},{2,6},{3,7},{4,0},{5,1},{6,2},{7,3},{8,12},{9,13},{10,... | collective-permute-start | bytes 49160 | tf_op jit(solution)/shard_map/ppermute | solution.py:674
  18.6 1.0 %copy-start.7 = (s32[16,32,256]{2,1,0:T(8,128)S(1)}, s32[16,32,256]{2,1,0:T(8,128)}, u32[]{:S(2)}) copy-start(s32[16,32,256]{2,1,0:T(8,128)} %refs_3_.1) | copy-start | bytes 1572868
  32.5 1.8 %collective-permute-start.5 = (f32[17,8,256]{2,1,0:T(8,128)S(1)}, f32[17,8,256]{2,1,0:T(8,128)S(1)}, u32[]{:S(2)}, u32[]{:S(2)}) collective-permute-start(f32[17,8,256]{2,1,0:T(8,128)S(1)} %get-tuple-element.29.refs_10_), channel_id=1, source_target_pairs={{0,1},{1,0},{2,3},{3,2},{4,5},{5,4},{6,7},{7,6},{8,9},{9,8},{10,11... | collective-permute-start | bytes 417800 | tf_op jit(solution)/shard_map/ppermute | solution.py:656
  34.4 5.7 %collective-permute-start.6 = (f32[17,8,256]{2,1,0:T(8,128)S(1)}, f32[17,8,256]{2,1,0:T(8,128)S(1)}, u32[]{:S(2)}, u32[]{:S(2)}) collective-permute-start(f32[17,8,256]{2,1,0:T(8,128)S(1)} %fusion.1), channel_id=1, source_target_pairs={{1,2},{2,1},{3,4},{4,3},{5,6},{6,5},{7,0},{0,7},{9,10},{10,9},{11,... | collective-permute-start | bytes 417800 | tf_op jit(solution)/shard_map/ppermute | solution.py:672
  35.4 12.0 %collective-permute-start.8 = (f32[7,32,256]{2,1,0:T(8,128)S(1)}, f32[7,32,256]{2,1,0:T(8,128)S(1)}, u32[]{:S(2)}, u32[]{:S(2)}) collective-permute-start(f32[7,32,256]{2,1,0:T(8,128)S(1)} %get-tuple-element.34.refs_8_), channel_id=1, source_target_pairs={{0,8},{8,0},{16,24},{24,16},{32,40},{40,32},{48,56},{56,48},{64,72... | collective-permute-start | bytes 688136 | tf_op jit(solution)/shard_map/ppermute | solution.py:656
  35.8 11.6 %collective-permute-start.9 = (f32[7,32,256]{2,1,0:T(8,128)S(1)}, f32[7,32,256]{2,1,0:T(8,128)S(1)}, u32[]{:S(2)}, u32[]{:S(2)}) collective-permute-start(f32[7,32,256]{2,1,0:T(8,128)S(1)} %get-tuple-element.35.refs_9_), channel_id=1, source_target_pairs={{8,16},{16,8},{24,32},{32,24},{40,48},{48,40},{56,64},{64,56},{72,... | collective-permute-start | bytes 688136 | tf_op jit(solution)/shard_map/ppermute | solution.py:656
  40.1 7.3 %collective-permute-start.7 = (f32[1,8,256]{2,1,0:T(8,128)S(1)}, f32[1,8,256]{2,1,0:T(8,128)S(1)}, u32[]{:S(2)}, u32[]{:S(2)}) collective-permute-start(f32[1,8,256]{2,1,0:T(8,128)S(1)} %slice_add_fusion.4), channel_id=1, source_target_pairs={{0,4},{1,5},{2,6},{3,7},{4,0},{5,1},{6,2},{7,3},{8,12},{9,13},{10,... | collective-permute-start | bytes 24584 | tf_op jit(solution)/shard_map/ppermute | solution.py:674
  51.6 1.4 %collective-permute-start.10 = (f32[17,8,256]{2,1,0:T(8,128)S(1)}, f32[17,8,256]{2,1,0:T(8,128)S(1)}, u32[]{:S(2)}, u32[]{:S(2)}) collective-permute-start(f32[17,8,256]{2,1,0:T(8,128)S(1)} %get-tuple-element.36.refs_11_), channel_id=1, source_target_pairs={{0,1},{1,0},{2,3},{3,2},{4,5},{5,4},{6,7},{7,6},{8,9},{9,8},{10,11... | collective-permute-start | bytes 417800 | tf_op jit(solution)/shard_map/ppermute | solution.py:656
  53.0 5.7 %collective-permute-start.11 = (f32[17,8,256]{2,1,0:T(8,128)S(1)}, f32[17,8,256]{2,1,0:T(8,128)S(1)}, u32[]{:S(2)}, u32[]{:S(2)}) collective-permute-start(f32[17,8,256]{2,1,0:T(8,128)S(1)} %fusion.2), channel_id=1, source_target_pairs={{1,2},{2,1},{3,4},{4,3},{5,6},{6,5},{7,0},{0,7},{9,10},{10,9},{11,... | collective-permute-start | bytes 417800 | tf_op jit(solution)/shard_map/ppermute | solution.py:672
  54.7 10.0 %collective-permute-start.13 = (f32[7,32,256]{2,1,0:T(8,128)S(1)}, f32[7,32,256]{2,1,0:T(8,128)S(1)}, u32[]{:S(2)}, u32[]{:S(2)}) collective-permute-start(f32[7,32,256]{2,1,0:T(8,128)S(1)} %get-tuple-element.40.refs_9_), channel_id=1, source_target_pairs={{0,8},{8,0},{16,24},{24,16},{32,40},{40,32},{48,56},{56,48},{64,72... | collective-permute-start | bytes 688136 | tf_op jit(solution)/shard_map/ppermute | solution.py:656
  54.7 11.5 %collective-permute-start.14 = (f32[7,32,256]{2,1,0:T(8,128)S(1)}, f32[7,32,256]{2,1,0:T(8,128)S(1)}, u32[]{:S(2)}, u32[]{:S(2)}) collective-permute-start(f32[7,32,256]{2,1,0:T(8,128)S(1)} %get-tuple-element.41.refs_10_), channel_id=1, source_target_pairs={{8,16},{16,8},{24,32},{32,24},{40,48},{48,40},{56,64},{64,56},{72,... | collective-permute-start | bytes 688136 | tf_op jit(solution)/shard_map/ppermute | solution.py:656
  58.7 6.0 %collective-permute-start.12 = (f32[1,8,256]{2,1,0:T(8,128)S(1)}, f32[1,8,256]{2,1,0:T(8,128)S(1)}, u32[]{:S(2)}, u32[]{:S(2)}) collective-permute-start(f32[1,8,256]{2,1,0:T(8,128)S(1)} %slice_add_fusion.2), channel_id=1, source_target_pairs={{0,4},{1,5},{2,6},{3,7},{4,0},{5,1},{6,2},{7,3},{8,12},{9,13},{10,... | collective-permute-start | bytes 24584 | tf_op jit(solution)/shard_map/ppermute | solution.py:674
